TPU v7x, 128 devices: a whole 4x4x4 slice. The times are simulated.
128 devices in a mesh: mode: 8 (over y_hi, x), space: 16 (over z, y_lo, core).
Axes of the slice: x: 4, y: 4 (y_hi: 2, y_lo: 2; y = y_hi * 2 + y_lo), z: 4, core: 2. Of those that a mesh axis runs over, the one named last changes fastest.
Arguments:
- resident: bfloat16 [2, 8192, 8, 4096], P(None, 'mode', None, 'space'), may hold values from -0.0625 to 0.0625
- source: bfloat16 [2, 768, 8, 4096], P(None, 'mode', None, 'space'), may hold values from -6 to 6
- insertion: bfloat16 [4, 768, 1024], replicated, may hold values from -0.21875 to 0.21875
- owners: int32 [256, 1], P('mode'), may hold values from 0 to 15; in each aligned block of 32 rows (0 to 31, 32 to 63, ...) at most 4 rows name the same one
- diag_time: int32 [4], replicated, may hold values from 0 to 7
- diag_mom: int32 [4], replicated, may hold values from 1 to 4
Outputs:
- mesons: bfloat16 [64, 2, 1024, 1024], P('space', None, 'mode')
Inputs may be any that keep to these rules, and one draw needn't show every extreme that they name: `owners`: within the 32 strips of one index of mode, no owner is named more than 4 times.
All inputs are finite; a program needn't handle non-finite values.
Results may differ from a plain program's by a relative error of at most 0.019.
Values may be sent and summed in bfloat16 or wider, within the bound.
No kernel may reach another device: no remote copies, remote signals or barrier semaphores. Data moves between devices by JAX's collectives and lax.ppermute only.
A program may use at most 192 MiB of HBM per device.

v0:
```python
import math

import jax
import jax.numpy as jnp
from jax import lax
from jax.sharding import PartitionSpec as P

STRIP = 128
LX = 96
CAP = 4


def phase_pair(diag_mom, start, count):
    lattice_positions = (start + jnp.arange(count, dtype=jnp.int32)) % LX
    turns = diag_mom[:, None] * lattice_positions[None, :] % LX
    angle = 2.0 * math.pi / LX * turns.astype(jnp.float32)
    return (jnp.cos(angle), jnp.sin(angle))


def on_device(resident, source, insertion, owners, diag_time, diag_mom):
    res_dev = resident.shape[1]
    slab = resident.shape[3]
    src_dev = source.shape[1]
    n_mode = lax.axis_size("mode")
    n_space = lax.axis_size("space")
    diagrams = insertion.shape[0]
    blocks = res_dev // STRIP
    strip_count = diagrams * blocks
    me_space = lax.axis_index("space")
    cosine, sine = phase_pair(diag_mom, me_space * slab, slab)
    res_slices = jnp.take(resident, diag_time, axis=2).astype(jnp.float32)
    real_in = res_slices[0] * cosine[None, :, :] - res_slices[1] * sine[None, :, :]
    imag_in = -(res_slices[0] * sine[None, :, :] + res_slices[1] * cosine[None, :, :])
    phased = jnp.stack([real_in, imag_in]).astype(jnp.bfloat16)
    portion_ranges = jnp.take(lax.all_gather(source, "mode", axis=1, tiled=True), diag_time, axis=2)
    combos = jnp.einsum(
        "prdx,qsdx->dpqrs", phased, portion_ranges, preferred_element_type=jnp.float32
    )
    real_out = combos[:, 0, 0] - combos[:, 1, 1]
    imag_out = combos[:, 0, 1] + combos[:, 1, 0]
    block_field = jnp.stack([real_out, imag_out], axis=1)
    band_list = block_field.astype(jnp.bfloat16).reshape(
        diagrams, 2, blocks, STRIP, src_dev * n_mode
    )
    band_list = band_list.transpose(0, 2, 1, 3, 4).reshape(strip_count, 2, STRIP, src_dev * n_mode)
    owner_list = owners[:, 0]
    same = owner_list[:, None] == owner_list[None, :]
    order = jnp.arange(strip_count, dtype=jnp.int32)
    earlier = order[None, :] < order[:, None]
    rank = jnp.sum((same & earlier).astype(jnp.int32), axis=1)
    slot = owner_list * CAP + rank
    slot_numbers = jnp.arange(n_space * CAP, dtype=jnp.int32)
    match = slot[None, :] == slot_numbers[:, None]
    filled = jnp.any(match, axis=1)
    slot_strip = jnp.sum(jnp.where(match, order[None, :], 0), axis=1)
    my_strip = lax.dynamic_slice_in_dim(slot_strip, me_space * CAP, CAP)
    local_completed = lax.dynamic_slice_in_dim(filled, me_space * CAP, CAP)
    outgoing = jnp.where(
        filled[:, None, None, None],
        jnp.take(band_list, slot_strip, axis=0),
        jnp.zeros((), jnp.bfloat16),
    )
    spatial_total = (
        lax.psum_scatter(outgoing, "space", scatter_dimension=0, tiled=True)
        .astype(jnp.float32)
        .astype(jnp.bfloat16)
    )
    selected_targets = jnp.take(insertion, my_strip // blocks, axis=0)
    product = jnp.einsum(
        "tkxf,tfq->tkxq", spatial_total, selected_targets, preferred_element_type=jnp.float32
    ).astype(jnp.bfloat16)
    mesons = jnp.where(local_completed[:, None, None, None], product, jnp.zeros_like(product))
    return mesons


def solution(mesh):
    in_specs = (
        P(None, "mode", None, "space"),
        P(None, "mode", None, "space"),
        P(),
        P("mode", None),
        P(),
        P(),
    )
    out_specs = P("space", None, "mode", None)
    return jax.shard_map(
        on_device, mesh=mesh, in_specs=in_specs, out_specs=out_specs, check_vma=False
    )
```

profile of v0, /device:TPU:1, one launch (start us, length us, event | category | flops | bytes accessed | tf_op | source)
XLA Modules:
  0.0 490.0 jit_solution(14932807228032636263)
XLA Ops:
  6.5 0.0 all-gather.2.cloned.1.call-start
  6.5 2.2 copy.13
  8.8 0.0 all-gather.2.cloned.1.call-update
  8.8 0.0 reduce-scatter.2.cloned.1.call-start
  8.8 0.0 copy-start.2
  8.9 12.2 %copy.14 = bf16[2,1024,8,256]{1,3,0,2:T(8,128)(2,1)} copy(bf16[2,1024,8,256]{3,2,1,0:T(8,128)(2,1)} %param.6) | data formatting | bytes 16777216 | tf_op args[0]
  21.1 0.0 copy-done.2
  21.1 6.8 %gather_fusion.1 = bf16[4,2,1024,256]{2,3,1,0:T(8,128)(2,1)} fusion(bf16[2,1024,8,256]{1,3,0,2:T(8,128)(2,1)} %copy.14, s32[1024]{0:T(1024)S(1)} %pad_clamp_fusion.2), kind=kCustom, calls=%fused_computation.1 | custom fusion | bytes 8388624 | tf_op jit(solution)/shard_map/jit(_take)/gather | solution.py:31
  27.9 6.2 %copy.15 = bf16[4,2,1024,256]{3,2,1,0:T(8,128)(2,1)} copy(bf16[4,2,1024,256]{2,3,1,0:T(8,128)(2,1)} %gather_fusion.1) | data formatting | bytes 8388608 | tf_op jit(solution)/shard_map/jit(_take)/gather | solution.py:31
  34.1 0.0 copy-done.1
  34.1 0.2 convert_reduce_fusion
  34.3 0.1 select_reduce_fusion
  34.4 0.1 fusion.15
  34.5 0.0 copy-done
  34.6 0.1 fusion.23
  34.7 2.8 convert_bitcast_fusion
  37.5 3.2 subtract_convert_fusion
  40.7 61.3 %all-gather.2.cloned.1.call-done = bf16[2,768,8,256]{3,1,2,0:T(8,128)(2,1)} async-done(((bf16[2,96,8,256]{3,1,2,0:T(8,128)(2,1)}), bf16[2,768,8,256]{3,1,2,0:T(8,128)(2,1)}) %all-gather.2.cloned.1.call-update) | async-done | bytes 6291472 | tf_op jit(solution)/shard_map/all_gather | solution.py:35
  102.0 3.5 gather_fusion
  105.5 20.7 %convolution_bitcast_fusion = f32[4,2,2,1024,768]{3,4,1,2,0:T(8,128)} fusion(bf16[1,1024,4,256]{3,1,0,2:T(8,128)(2,1)} %get-tuple-element.10, bf16[1,1024,4,256]{3,1,0,2:T(8,128)(2,1)} %get-tuple-element.9, bf16[4,2,768,256]{3,2,1,0:T(8,128)(2,1)S(1)} %gather_fusion, pred[4]{0:T(512)(128)(4,1)S(1)} %compare_and_fusion.1), kind=kOutput, calls=%fused_computation.5 | convolution fusion | flops 6452412416 | bytes 57671684 | tf_op jit(solution)/shard_map/prdx,qsdx->dpqrs/dot_general | solution.py:36
  126.2 22.2 %fusion.1 = (bf16[4,1,1,1024,768]{3,4,1,2,0:T(8,128)(2,1)}, bf16[4,1,1,1024,768]{3,4,1,2,0:T(8,128)(2,1)}) fusion(f32[4,2,2,1024,768]{3,4,1,2,0:T(8,128)} %convolution_bitcast_fusion), kind=kLoop, calls=%fused_computation.9 | loop fusion | flops 12582912 | bytes 62914560 | tf_op jit(solution)/shard_map/convert.3
  148.5 8.7 %copy.21 = bf16[4,1,1,1024,768]{4,3,0,2,1:T(8,128)(2,1)} copy(bf16[4,1,1,1024,768]{3,4,1,2,0:T(8,128)(2,1)} %get-tuple-element.7) | data formatting | bytes 12582912 | tf_op jit(solution)/shard_map/sub | solution.py:39
  157.1 8.6 %copy.22 = bf16[4,1,1,1024,768]{4,3,0,2,1:T(8,128)(2,1)} copy(bf16[4,1,1,1024,768]{3,4,1,2,0:T(8,128)(2,1)} %get-tuple-element.8) | data formatting | bytes 12582912 | tf_op jit(solution)/shard_map/add | solution.py:40
  165.8 10.7 %pad_maximum_fusion = bf16[4,2,8,128,768]{4,3,1,2,0:T(8,128)(2,1)} fusion(bf16[4,1,8,128,768]{4,3,1,2,0:T(8,128)(2,1)} %bitcast.37, bf16[4,1,8,128,768]{4,3,1,2,0:T(8,128)(2,1)} %bitcast.36), kind=kLoop, calls=%fused_computation.10 | loop fusion | flops 6291456 | bytes 25165824 | tf_op jit(solution)/shard_map/stack | solution.py:41
  176.5 14.8 %gather_fusion.2 = bf16[64,2,128,768]{3,2,1,0:T(8,128)(2,1)} fusion(bf16[32,2,128,768]{3,2,1,0:T(8,128)(2,1)} %bitcast.35, s32[1024]{0:T(1024)S(1)} %pad_clamp_fusion.1), kind=kCustom, calls=%fused_computation.2 | custom fusion | bytes 50331904 | tf_op jit(solution)/shard_map/jit(_take)/gather | solution.py:60
  191.3 21.6 %select_select_fusion = bf16[64,2,128,768]{3,2,1,0:T(8,128)(2,1)} fusion(bf16[64,2,128,768]{3,2,1,0:T(8,128)(2,1)} %gather_fusion.2, pred[64]{0:T(512)(128)(4,1)S(1)} %compare_and_fusion.2, pred[64]{0:T(512)(128)(4,1)S(1)} %fusion.15), kind=kLoop, calls=%fused_computation.4 | loop fusion | flops 25165824 | bytes 50331776 | tf_op jit(solution)/shard_map/jit(_where)/select_n | solution.py:58
  212.9 0.0 reduce-scatter.2.cloned.1.call-update
  213.0 0.1 dynamic_slice.6
  213.0 0.1 compare_and_fusion
  213.1 6.4 %gather_fusion.3 = bf16[4,768,1024]{2,1,0:T(8,128)(2,1)} fusion(bf16[4,768,1024]{2,1,0:T(8,128)(2,1)} %param.8, s32[1024]{0:T(1024)S(1)} %pad_clamp_fusion), kind=kCustom, calls=%fused_computation.3 | custom fusion | bytes 12582928 | tf_op jit(solution)/shard_map/jit(_take)/gather | solution.py:68
  219.6 257.1 %reduce-scatter.2.cloned.1.call-done = bf16[4,2,128,768]{3,2,1,0:T(8,128)(2,1)} async-done(((bf16[64,2,128,768]{3,2,1,0:T(8,128)(2,1)}), bf16[4,2,128,768]{3,2,1,0:T(8,128)(2,1)}) %reduce-scatter.2.cloned.1.call-update) | async-done | bytes 1572880 | tf_op jit(solution)/shard_map/reduce_scatter | solution.py:64
  476.7 6.5 %convert_select_fusion = bf16[4,2,128,1024]{3,2,1,0:T(8,128)(2,1)} fusion(pred[4]{0:T(512)(128)(4,1)S(1)} %dynamic_slice.6, bf16[4,2,128,768]{3,2,1,0:T(8,128)(2,1)} %reduce-scatter.2.cloned.1.call-done, bf16[4,768,1024]{2,1,0:T(8,128)(2,1)} %gather_fusion.3, pred[4]{0:T(512)(128)(4,1)S(1)} %get-tuple-element.5), kind=kOutput, calls=%fused_computation.25 | convolution fusion | flops 1615855616 | bytes 9961480 | tf_op jit(solution)/shard_map/tkxf,tfq->tkxq/dot_general | solution.py:69
  (11 shorter events, 0.1 us)
Async XLA Ops:
  6.5 95.5 %all-gather.2.cloned.1.call-start = ((), (), s32[]{:S(2)}) async-start(), calls=%async_computation.1 | async-start | bytes 7077888 | tf_op jit(solution)/shard_map/all_gather | solution.py:35
  8.8 467.9 %reduce-scatter.2.cloned.1.call-start = ((), (), s32[]{:S(2)}) async-start(), calls=%async_computation.2 | async-start | bytes 26738688 | tf_op jit(solution)/shard_map/reduce_scatter | solution.py:64
  8.8 12.2 %copy-start.2 = (s32[4]{0:T(128)S(1)}, s32[4]{0:T(128)}, u32[]{:S(2)}) copy-start(s32[4]{0:T(128)} %param.10) | copy-start | bytes 52
  27.9 6.3 %copy-start.1 = (s32[32,1]{0,1:T(1,128)S(1)}, s32[32,1]{0,1:T(1,128)}, u32[]{:S(2)}) copy-start(s32[32,1]{0,1:T(1,128)} %param.9) | copy-start | bytes 388
  27.9 6.7 %copy-start = (s32[4]{0:T(128)S(1)}, s32[4]{0:T(128)}, u32[]{:S(2)}) copy-start(s32[4]{0:T(128)} %param.11) | copy-start | bytes 52
Sparse Core Ops, SparseCore 0:
  9.6 92.3 all-gather.1
  213.1 263.5 reduce-scatter.1
where the time goes:
time: 492 us; the launch traced here: 490 us
  waiting for transfers between devices  318 us (65%)
  local copies, waits for them, and re-layouts  69.7 us (14%)
  other arithmetic  61.2 us (12%)
  matrix products  27.1 us (6%)
  between operations  13.5 us (3%)
    reduce_scatter x1, waiting for transfers between devices, on_device(): lax.psum_scatter(outgoing, 'space', scatter_dimension=0, tiled=True)  257 us
    all_gather x1, waiting for transfers between devices, on_device(): lax.all_gather(source, 'mode', axis=1, tiled=True)  61.3 us
    another operation x2, other arithmetic  25.5 us
    select_n x1, other arithmetic, on_device(): jnp.where(filled[:, None, None, None], jnp.take(band_list, slot_strip, ax...  21.6 us
    dot_general x1, matrix products, on_device(): jnp.einsum('prdx,qsdx->dpqrs', phased, portion_ranges, preferred_element_...  20.7 us
    gather x1, local copies, waits for them, and re-layouts, on_device(): jnp.take(band_list, slot_strip, axis=0)  14.8 us
    unnamed x8, local copies, waits for them, and re-layouts  14.5 us
    gather x2, local copies, waits for them, and re-layouts, on_device(): res_slices = jnp.take(resident, diag_time, axis=2).astype(jnp.float32)  13 us
  transfers between devices with their start and end apart: 2, of which 2 were waited for; matrix products, arithmetic and copies ran while one was open for 8% of the time, Pallas kernels for 0%

commit v1 on v0

v1 whole, which is shorter than its diff:
```python
import functools
import math

import jax
import jax.numpy as jnp
from jax import lax
from jax.experimental import pallas as pl
from jax.experimental.pallas import tpu as pltpu
from jax.sharding import PartitionSpec as P

STRIP = 128
LX = 96
CAP = 4
BF = jnp.bfloat16
F32 = jnp.float32
VMEM_LIMIT = 48 * 1024 * 1024


def phase_pair(diag_mom, start, count):
    lattice_positions = (start + jnp.arange(count, dtype=jnp.int32)) % LX
    turns = diag_mom[:, None] * lattice_positions[None, :] % LX
    angle = 2.0 * math.pi / LX * turns.astype(F32)
    return jnp.cos(angle), jnp.sin(angle)


def params():
    return pltpu.CompilerParams(vmem_limit_bytes=VMEM_LIMIT)


def cost(flops, size):
    return pl.CostEstimate(flops=flops, bytes_accessed=size, transcendentals=0)


LANES = 128


def widen(ref, wide):
    parts, rows, times, _ = ref.shape
    for p in range(parts):
        for h in range(wide.shape[1]):
            x = ref[p, :, :, h * LANES : (h + 1) * LANES]
            wide[p, h] = x.astype(F32).reshape(rows * times, LANES)


def narrow(wide, p, rows):
    return jnp.concatenate([wide[p, h, rows, :] for h in range(wide.shape[1])], axis=1)


def source_kernel(meta, cos_ref, sin_ref, src_ref, keep_ref, send_ref, wide):
    parts, modes, times, sites = src_ref.shape
    half = modes // 2
    widen(src_ref, wide)
    core = meta[5]
    for d in range(keep_ref.shape[0]):
        c = cos_ref[d : d + 1, :]
        s = sin_ref[d : d + 1, :]
        for ref, who in ((keep_ref, core), (send_ref, 1 - core)):
            rows = pl.ds(who * (half * times) + meta[d], half, stride=times)
            re = narrow(wide, 0, rows)
            im = narrow(wide, 1, rows)
            ref[d, :, 0:sites] = (re * c + im * s).astype(BF)
            ref[d, :, sites : 2 * sites] = (im * c - re * s).astype(BF)


def source_slices(meta, cosine, sine, source):
    parts, modes, times, sites = source.shape
    diagrams = cosine.shape[0]
    piece = jax.ShapeDtypeStruct((diagrams, modes // 2, parts * sites), BF)
    return pl.pallas_call(
        source_kernel,
        out_shape=(piece, piece),
        in_specs=[pl.BlockSpec(memory_space=pltpu.SMEM)]
        + [pl.BlockSpec(memory_space=pltpu.VMEM)] * 3,
        out_specs=[pl.BlockSpec(memory_space=pltpu.VMEM)] * 2,
        scratch_shapes=[pltpu.VMEM((parts, sites // LANES, modes * times, LANES), F32)],
        compiler_params=params(),
        cost_estimate=cost(10**6, 2 * 10**6),
        name="source_slices",
    )(meta, cosine, sine, source)


def resident_kernel(meta, res_ref, out_ref, wide):
    parts, strip, times, sites = res_ref.shape
    diagrams, groups, _, rows, _ = out_ref.shape
    widen(res_ref, wide)
    for d in range(diagrams):
        for p in range(parts):
            x = narrow(wide, p, pl.ds(meta[d], strip, stride=times)).astype(BF)
            for g in range(groups):
                out_ref[d, g ^ meta[4], 0, :, p * sites : (p + 1) * sites] = x[
                    g * rows : (g + 1) * rows
                ]


def resident_slices(meta, resident, diagrams, groups):
    parts, res_dev, times, sites = resident.shape
    blocks = res_dev // STRIP
    rows = STRIP // groups
    return pl.pallas_call(
        resident_kernel,
        out_shape=jax.ShapeDtypeStruct(
            (diagrams, groups, blocks, rows, parts * sites), BF
        ),
        grid_spec=pltpu.PrefetchScalarGridSpec(
            num_scalar_prefetch=1,
            grid=(blocks,),
            in_specs=[
                pl.BlockSpec((parts, STRIP, times, sites), lambda b, meta: (0, b, 0, 0))
            ],
            out_specs=pl.BlockSpec(
                (diagrams, groups, 1, rows, parts * sites),
                lambda b, meta: (0, 0, b, 0, 0),
            ),
            scratch_shapes=[pltpu.VMEM((parts, sites // LANES, STRIP * times, LANES), F32)],
        ),
        compiler_params=params(),
        cost_estimate=cost(10**7, 13 * 10**6),
        name="resident_slices",
    )(meta, resident)


def field_kernel(
    meta, own_ref, par_ref, a0, a1, a2, b0, b1, b2,
    a_keep, a_send, b_keep, b_send, real_rhs, imag_rhs,
):
    j = pl.program_id(0)
    me = meta[6]
    pieces = (
        ((a0, (0, 4)), (a1, (1, 5)), (a2, (3, 7, 2, 6))),
        ((b0, (0, 4)), (b1, (3, 7)), (b2, (1, 5, 2, 6))),
    )
    modes, width = a0.shape[1:]
    sites = width // 2

    @pl.when(j == 0)
    def _():
        for side, arrays in enumerate(pieces):
            for ref, places in arrays:
                for n, place in enumerate(places):
                    v = ref[n]
                    at = me ^ place
                    real_rhs[side, at] = v
                    imag_rhs[side, at, :, 0:sites] = v[:, sites:]
                    imag_rhs[side, at, :, sites:] = -v[:, 0:sites]

    rows = own_ref.shape[1] * own_ref.shape[2] * own_ref.shape[3]
    own = own_ref[0].reshape(rows, width)
    par = par_ref[0].reshape(rows, width)

    def product(rhs):
        dims = (((1,), (1,)), ((), ()))
        columns = rhs.shape[1] * rhs.shape[2]
        return (
            lax.dot_general(own, rhs[0].reshape(columns, width), dims, preferred_element_type=F32)
            + lax.dot_general(par, rhs[1].reshape(columns, width), dims, preferred_element_type=F32)
        ).astype(BF)

    real = product(real_rhs)
    imag = product(imag_rhs)
    for step, (ra, na, rb, nb) in enumerate(
        ((a_keep, 0, b_keep, 0), (a_send, 0, b_keep, 1), (a_send, 1, b_send, 1), (a_keep, 1, b_send, 0))
    ):

        @pl.when(j == step)
        def _(ra=ra, na=na, rb=rb, nb=nb):
            ra[na] = real
            rb[nb] = imag


def partial_field(d, meta, own, par, side_a, side_b):
    groups, blocks, rows, width = own.shape[1:]
    pair = groups // 4
    modes = side_a[0].shape[1]
    columns = 8 * modes
    out = jax.ShapeDtypeStruct((2, pair * blocks * rows, columns), BF)
    res_spec = pl.BlockSpec(
        (1, pair, blocks, rows, width), lambda j, meta: (d, j, 0, 0, 0)
    )

    def whole(x):
        return pl.BlockSpec(x.shape, lambda j, meta: (0,) * len(x.shape))

    return pl.pallas_call(
        field_kernel,
        out_shape=(out,) * 4,
        grid_spec=pltpu.PrefetchScalarGridSpec(
            num_scalar_prefetch=1,
            grid=(4,),
            in_specs=[res_spec, res_spec] + [whole(x) for x in (*side_a, *side_b)],
            out_specs=[whole(out)] * 4,
            scratch_shapes=[pltpu.VMEM((2, 8, modes, width), BF)] * 2,
        ),
        compiler_params=params(),
        cost_estimate=cost(2 * 1024 * 1024 * 768, 5 * 10**6),
        name=f"field_{d}",
    )(meta, own, par, *side_a, *side_b)


def pack_kernel(diagrams, slot_ref, *refs):
    ins, out_ref, strips = refs[: 3 * diagrams], refs[3 * diagrams], refs[-1]
    blocks = strips.shape[0] // diagrams
    rows, columns = strips.shape[2:]
    for d in range(diagrams):
        own_a, own_b, other = ins[3 * d : 3 * d + 3]
        for p, own in enumerate((own_a, own_b)):
            total = (own[...] + other[p].astype(F32)).astype(BF)
            strips[d * blocks : (d + 1) * blocks, p] = total.reshape(
                blocks, rows, columns
            )

    def one(slot, carry):
        out_ref[slot] = strips[slot_ref[slot]]
        return carry

    lax.fori_loop(0, out_ref.shape[0], one, 0)


def pack(slot_strip, finished, blocks):
    diagrams = len(finished)
    tall, columns = finished[0][0].shape
    rows = tall // blocks
    flat = [x for triple in finished for x in triple]
    return pl.pallas_call(
        functools.partial(pack_kernel, diagrams),
        out_shape=jax.ShapeDtypeStruct((slot_strip.shape[0], 2, rows, columns), BF),
        in_specs=[pl.BlockSpec(memory_space=pltpu.SMEM)]
        + [pl.BlockSpec(memory_space=pltpu.VMEM)] * len(flat),
        out_specs=pl.BlockSpec(memory_space=pltpu.VMEM),
        scratch_shapes=[pltpu.VMEM((diagrams * blocks, 2, rows, columns), BF)],
        compiler_params=params(),
        cost_estimate=cost(10**6, 4 * 10**6),
        name="pack",
    )(slot_strip, *flat)


def insertion_kernel(which, filled, rows_ref, ins_ref, out_ref):
    t = pl.program_id(0)
    columns = rows_ref.shape[-1]
    groups = rows_ref.shape[0] // 2
    width = ins_ref.shape[-1]

    @pl.when(filled[t] == 0)
    def _():
        out_ref[...] = jnp.zeros_like(out_ref)

    @pl.when(filled[t] != 0)
    def _():
        total = None
        for core in range(2):
            lhs = jnp.concatenate(
                [rows_ref[2 * g + core, 0, p] for p in range(2) for g in range(groups)],
                axis=0,
            )
            rhs = ins_ref[0, :, core].reshape(columns, width)
            term = jnp.dot(lhs, rhs, preferred_element_type=F32)
            total = term if total is None else total + term
        out_ref[0] = total.astype(BF).reshape(2, STRIP, width)


def contract(which, filled, received, insertion):
    senders, cap, parts, rows, columns = received.shape
    diagrams, _, width = insertion.shape
    n_mode = 8
    modes = columns // n_mode
    split = insertion.reshape(diagrams, n_mode, 2, modes, width)
    return pl.pallas_call(
        insertion_kernel,
        out_shape=jax.ShapeDtypeStruct((cap, parts, STRIP, width), BF),
        grid_spec=pltpu.PrefetchScalarGridSpec(
            num_scalar_prefetch=2,
            grid=(cap,),
            in_specs=[
                pl.BlockSpec(
                    (senders, 1, parts, rows, columns), lambda t, w, f: (0, t, 0, 0, 0)
                ),
                pl.BlockSpec(
                    (1, n_mode, 2, modes, width), lambda t, w, f: (w[t], 0, 0, 0, 0)
                ),
            ],
            out_specs=pl.BlockSpec(
                (1, parts, STRIP, width), lambda t, w, f: (t, 0, 0, 0)
            ),
        ),
        compiler_params=params(),
        cost_estimate=cost(16 * 10**8, 10**7),
        name="contract",
    )(which, filled, received, split)


def swap(x, axis, bits):
    n = lax.axis_size(axis)
    return lax.ppermute(x, axis, [(i, i ^ bits) for i in range(n)])


Z1, Z3, Y1, CORE = 4, 12, 2, 1
X1, X3, YHI = 1, 3, 4


def slots(owner_list, n_space, me_space):
    strip_count = owner_list.shape[0]
    same = owner_list[:, None] == owner_list[None, :]
    order = jnp.arange(strip_count, dtype=jnp.int32)
    earlier = order[None, :] < order[:, None]
    rank = jnp.sum((same & earlier).astype(jnp.int32), axis=1)
    slot = owner_list * CAP + rank
    numbers = jnp.arange(n_space * CAP, dtype=jnp.int32)
    match = slot[None, :] == numbers[:, None]
    slot_strip = jnp.sum(jnp.where(match, order[None, :], 0), axis=1)
    mine = me_space * CAP + jnp.arange(CAP, dtype=jnp.int32)
    my_match = slot[None, :] == mine[:, None]
    my_strip = jnp.sum(jnp.where(my_match, order[None, :], 0), axis=1)
    filled = jnp.sum(my_match.astype(jnp.int32), axis=1)
    return slot_strip, my_strip, filled


def on_device(resident, source, insertion, owners, diag_time, diag_mom):
    slab = resident.shape[3]
    n_space = lax.axis_size("space")
    diagrams = insertion.shape[0]
    blocks = resident.shape[1] // STRIP
    me_space = lax.axis_index("space")
    me_mode = lax.axis_index("mode")
    meta = jnp.concatenate(
        [diag_time, jnp.stack([me_space // 2, me_space % 2, me_mode]).astype(jnp.int32)]
    )
    cosine, sine = phase_pair(diag_mom, me_space * slab, slab)

    keep, send = source_slices(meta, cosine, sine, source)
    arrived = swap(send, "space", CORE)
    own = resident_slices(meta, resident, diagrams, n_space // 2)
    par = swap(own, "space", CORE)
    slot_strip, my_strip, filled = slots(owners[:, 0], n_space, me_space)

    finished = []
    for d in range(diagrams):
        pair = jnp.stack([keep[d], arrived[d]])
        far = swap(pair, "mode", YHI)
        a0 = jnp.stack([pair[0], far[0]])
        b0 = jnp.stack([pair[1], far[1]])
        a1 = swap(a0, "mode", X1)
        b1 = swap(b0, "mode", X3)
        a2 = swap(jnp.concatenate([a0, a1]), "mode", X3)
        b2 = swap(jnp.concatenate([b0, b1]), "mode", X1)
        a_keep, a_send, b_keep, b_send = partial_field(
            d, meta, own, par, (a0, a1, a2), (b0, b1, b2)
        )
        a_in = swap(a_send, "space", Z1)
        b_in = swap(b_send, "space", Z3)
        a_pass = (a_keep[1].astype(F32) + a_in[1].astype(F32)).astype(BF)
        b_pass = (b_keep[1].astype(F32) + b_in[1].astype(F32)).astype(BF)
        a_last = swap(a_pass, "space", Z3)
        b_last = swap(b_pass, "space", Z1)
        a_sum = a_keep[0].astype(F32) + a_in[0].astype(F32) + a_last.astype(F32)
        b_sum = b_keep[0].astype(F32) + b_in[0].astype(F32) + b_last.astype(F32)
        tall = a_sum.shape[0] // 2
        over_y = swap(jnp.stack([a_sum[tall:], b_sum[tall:]]).astype(BF), "space", Y1)
        finished.append((a_sum[:tall], b_sum[:tall], over_y))

    outgoing = pack(slot_strip, finished, blocks)
    outgoing = outgoing.reshape(n_space, CAP, *outgoing.shape[1:])
    received = lax.all_to_all(outgoing, "space", 0, 0, tiled=True)
    return contract(my_strip // blocks, filled, received, insertion)


def solution(mesh):
    in_specs = (
        P(None, "mode", None, "space"),
        P(None, "mode", None, "space"),
        P(),
        P("mode", None),
        P(),
        P(),
    )
    out_specs = P("space", None, "mode", None)
    return jax.shard_map(
        on_device, mesh=mesh, in_specs=in_specs, out_specs=out_specs, check_vma=False
    )
```

time: 492 us -> 162 us (0.33)
  waiting for transfers between devices: 318 us -> 58.2 us
  local copies, waits for them, and re-layouts: 69.7 us -> 0.3 us
  starting transfers between devices: 0.04 us -> 60.4 us
  other arithmetic: 61.2 us -> 2.72 us
  Pallas kernels: 0 us -> 38.4 us
  matrix products: 27.1 us -> 0 us
  between operations: 13.5 us -> 0.62 us
    reduce_scatter x1 -> x0, waiting for transfers between devices: 257 us -> none  [on_device(): lax.psum_scatter(outgoing, 'space', scatter_dimension=0, tiled=True)]
    all_gather x1 -> x0, waiting for transfers between devices: 61.3 us -> none  [on_device(): lax.all_gather(source, 'mode', axis=1, tiled=True)]
    ppermute x0 -> x42, starting transfers between devices: none -> 46.3 us  [swap(): return lax.ppermute(x, axis, [(i, i ^ bits) for i in range(n)])]
    pallas_call x0 -> x8, Pallas kernels: none -> 38.4 us  [the longest x4 20.4 us: partial_field(): pl.pallas_call(field_kernel, out_shape=(out,) * 4, grid_spec=pltpu.Prefet...]
    gather x5 -> x0, local copies, waits for them, and re-layouts: 37.8 us -> none  [the longest x1 14.8 us: on_device(): jnp.take(band_list, slot_strip, axis=0)]
    ppermute x0 -> x42, waiting for transfers between devices: none -> 36.8 us  [swap(): return lax.ppermute(x, axis, [(i, i ^ bits) for i in range(n)])]
    another operation x3 -> x16, other arithmetic: 36.2 us -> 0.25 us  [the longest x4 0.11 us: on_device(): jnp.stack([a_sum[tall:], b_sum[tall:]]).astype(BF)]
    dot_general x2 -> x0, matrix products: 27.1 us -> none  [the longest x1 20.7 us: on_device(): jnp.einsum('prdx,qsdx->dpqrs', phased, portion_ranges, preferred_element_...]
  transfers between devices with their start and end apart: 2 -> 43, of which waited for: 2 -> 19; matrix products, arithmetic and copies ran while one was open for 8% -> 1% of each run, Pallas kernels for 0% -> 13%
where the time goes in v1:
time: 162 us; the launch traced here: 161 us
  starting transfers between devices  60.4 us (37%)
  waiting for transfers between devices  58.2 us (36%)
  Pallas kernels  38.4 us (24%)
  other arithmetic  2.72 us (2%)
    ppermute x42, starting transfers between devices, swap(): return lax.ppermute(x, axis, [(i, i ^ bits) for i in range(n)])  46.3 us
    ppermute x42, waiting for transfers between devices, swap(): return lax.ppermute(x, axis, [(i, i ^ bits) for i in range(n)])  36.8 us
    all_to_all x1, waiting for transfers between devices, on_device(): received = lax.all_to_all(outgoing, 'space', 0, 0, tiled=True)  21.4 us
    pallas_call x4, Pallas kernels, partial_field(): pl.pallas_call(field_kernel, out_shape=(out,) * 4, grid_spec=pltpu.Prefet...  20.4 us
    all_to_all x1, starting transfers between devices, on_device(): received = lax.all_to_all(outgoing, 'space', 0, 0, tiled=True)  14.1 us
    pallas_call x1, Pallas kernels, resident_slices(): pl.pallas_call(resident_kernel, out_shape=jax.ShapeDtypeStruct((diagrams,...  9.47 us
    pallas_call x1, Pallas kernels, contract(): pl.pallas_call(insertion_kernel, out_shape=jax.ShapeDtypeStruct((cap, par...  5.33 us
  transfers between devices with their start and end apart: 43, of which 19 were waited for; matrix products, arithmetic and copies ran while one was open for 1% of the time, Pallas kernels for 13%

profile of v1, /device:TPU:1, one launch (start us, length us, event | category | flops | bytes accessed | tf_op | source)
XLA Modules:
  0.0 160.6 jit_solution(11140738505873304869)
XLA Ops:
  0.7 9.5 %resident_slices.1.own_ref = bf16[4,8,8,16,512]{4,3,2,1,0:T(8,128)(2,1)} custom-call(s32[7]{0:T(128)S(1)} %pad_add_fusion.meta, bf16[2,1024,8,256]{3,2,1,0:T(8,128)(2,1)} %res_ref.1), custom_call_target="tpu_custom_call" | custom-call | flops 10000000 | bytes 13000000 | tf_op jit(solution)/shard_map/resident_slices/pallas_call | solution.py:99
  13.0 5.7 %collective-permute-done.1 = bf16[4,48,512]{2,1,0:T(8,128)(2,1)S(1)} collective-permute-done((bf16[4,48,512]{2,1,0:T(8,128)(2,1)S(1)}, bf16[4,48,512]{2,1,0:T(8,128)(2,1)S(1)}, u32[]{:S(2)}, u32[]{:S(2)}) %collective-permute-start.1) | collective-permute-done | bytes 196640 | tf_op jit(solution)/shard_map/ppermute | solution.py:292
  18.7 3.1 %collective-permute-start.32 = (bf16[2,48,512]{2,1,0:T(8,128)(2,1)S(1)}, bf16[2,48,512]{2,1,0:T(8,128)(2,1)S(1)}, u32[]{:S(2)}, u32[]{:S(2)}) collective-permute-start(bf16[2,48,512]{2,1,0:T(8,128)(2,1)S(1)} %pad_maximum_fusion.18), channel_id=1, source_target_pairs={{0,64},{16,80},{32,96},{48,112},{64,0},{80,16},{96,32},{112,48},{1... | collective-permute-start | bytes 294920 | tf_op jit(solution)/shard_map/ppermute | solution.py:292
  21.9 3.0 %collective-permute-start.12 = (bf16[2,48,512]{2,1,0:T(8,128)(2,1)S(1)}, bf16[2,48,512]{2,1,0:T(8,128)(2,1)S(1)}, u32[]{:S(2)}, u32[]{:S(2)}) collective-permute-start(bf16[2,48,512]{2,1,0:T(8,128)(2,1)S(1)} %pad_maximum_fusion.14), channel_id=1, source_target_pairs={{0,64},{16,80},{32,96},{48,112},{64,0},{80,16},{96,32},{112,48},{1... | collective-permute-start | bytes 294920 | tf_op jit(solution)/shard_map/ppermute | solution.py:292
  25.1 2.6 %collective-permute-start.35 = (bf16[2,48,512]{2,1,0:T(8,128)(2,1)S(1)}, bf16[2,48,512]{2,1,0:T(8,128)(2,1)S(1)}, u32[]{:S(2)}, u32[]{:S(2)}) collective-permute-start(bf16[2,48,512]{2,1,0:T(8,128)(2,1)S(1)} %pad_maximum_fusion.23.b0), channel_id=1, source_target_pairs={{0,48},{16,32},{32,16},{48,0},{64,112},{80,96},{96,80},{112,64},{1... | collective-permute-start | bytes 294920 | tf_op jit(solution)/shard_map/ppermute | solution.py:292
  29.2 2.5 %collective-permute-start.25 = (bf16[2,48,512]{2,1,0:T(8,128)(2,1)S(1)}, bf16[2,48,512]{2,1,0:T(8,128)(2,1)S(1)}, u32[]{:S(2)}, u32[]{:S(2)}) collective-permute-start(bf16[2,48,512]{2,1,0:T(8,128)(2,1)S(1)} %pad_maximum_fusion.22.b0), channel_id=1, source_target_pairs={{0,48},{16,32},{32,16},{48,0},{64,112},{80,96},{96,80},{112,64},{1... | collective-permute-start | bytes 294920 | tf_op jit(solution)/shard_map/ppermute | solution.py:292
  32.7 1.9 %collective-permute-start.15 = (bf16[2,48,512]{2,1,0:T(8,128)(2,1)S(1)}, bf16[2,48,512]{2,1,0:T(8,128)(2,1)S(1)}, u32[]{:S(2)}, u32[]{:S(2)}) collective-permute-start(bf16[2,48,512]{2,1,0:T(8,128)(2,1)S(1)} %pad_maximum_fusion.21.b0), channel_id=1, source_target_pairs={{0,48},{16,32},{32,16},{48,0},{64,112},{80,96},{96,80},{112,64},{1... | collective-permute-start | bytes 294920 | tf_op jit(solution)/shard_map/ppermute | solution.py:292
  39.2 1.5 collective-permute-start.34
  43.8 1.6 collective-permute-done.34.a2
  45.4 2.2 %collective-permute-start.14 = (bf16[4,48,512]{2,1,0:T(8,128)(2,1)S(1)}, bf16[4,48,512]{2,1,0:T(8,128)(2,1)S(1)}, u32[]{:S(2)}, u32[]{:S(2)}) collective-permute-start(bf16[4,48,512]{2,1,0:T(8,128)(2,1)S(1)} %pad_maximum_fusion.3), channel_id=1, source_target_pairs={{0,48},{16,32},{32,16},{48,0},{64,112},{80,96},{96,80},{112,64},{1... | collective-permute-start | bytes 589832 | tf_op jit(solution)/shard_map/ppermute | solution.py:292
  47.5 5.1 %field_3.1 = (bf16[2,256,384]{2,1,0:T(8,128)(2,1)S(1)}, bf16[2,256,384]{2,1,0:T(8,128)(2,1)S(1)}, bf16[2,256,384]{2,1,0:T(8,128)(2,1)S(1)}, bf16[2,256,384]{2,1,0:T(8,128)(2,1)S(1)}) custom-call(s32[7]{0:T(128)S(1)} %pad_add_fusion.meta, bf16[4,8,8,16,512]{4,3,2,1,0:T(8,128)(2,1)} %resident_slices.1.own_ref, ...), custom_call_target="tpu_custom_call" | custom-call | flops 1610612736 | bytes 5000000 | tf_op jit(solution)/shard_map/field_3/pallas_call | solution.py:183
  53.3 3.8 %collective-permute-start.39 = (bf16[2,256,384]{2,1,0:T(8,128)(2,1)S(1)}, bf16[2,256,384]{2,1,0:T(8,128)(2,1)S(1)}, u32[]{:S(2)}, u32[]{:S(2)}) collective-permute-start(bf16[2,256,384]{2,1,0:T(8,128)(2,1)S(1)} %get-tuple-element.40), channel_id=1, source_target_pairs={{0,12},{1,13},{2,14},{3,15},{4,8},{5,9},{6,10},{7,11},{8,4},{9,5},... | collective-permute-start | bytes 1179656 | tf_op jit(solution)/shard_map/ppermute | solution.py:292
  57.0 5.1 %field_2.1 = (bf16[2,256,384]{2,1,0:T(8,128)(2,1)S(1)}, bf16[2,256,384]{2,1,0:T(8,128)(2,1)S(1)}, bf16[2,256,384]{2,1,0:T(8,128)(2,1)S(1)}, bf16[2,256,384]{2,1,0:T(8,128)(2,1)S(1)}) custom-call(s32[7]{0:T(128)S(1)} %pad_add_fusion.meta, bf16[4,8,8,16,512]{4,3,2,1,0:T(8,128)(2,1)} %resident_slices.1.own_ref, ...), custom_call_target="tpu_custom_call" | custom-call | flops 1610612736 | bytes 5000000 | tf_op jit(solution)/shard_map/field_2/pallas_call | solution.py:183
  62.4 5.1 %field_1.1 = (bf16[2,256,384]{2,1,0:T(8,128)(2,1)S(1)}, bf16[2,256,384]{2,1,0:T(8,128)(2,1)S(1)}, bf16[2,256,384]{2,1,0:T(8,128)(2,1)S(1)}, bf16[2,256,384]{2,1,0:T(8,128)(2,1)S(1)}) custom-call(s32[7]{0:T(128)S(1)} %pad_add_fusion.meta, bf16[4,8,8,16,512]{4,3,2,1,0:T(8,128)(2,1)} %resident_slices.1.own_ref, ...), custom_call_target="tpu_custom_call" | custom-call | flops 1610612736 | bytes 5000000 | tf_op jit(solution)/shard_map/field_1/pallas_call | solution.py:183
  67.5 1.4 collective-permute-start.27
  68.9 2.1 %collective-permute-start.19 = (bf16[2,256,384]{2,1,0:T(8,128)(2,1)S(1)}, bf16[2,256,384]{2,1,0:T(8,128)(2,1)S(1)}, u32[]{:S(2)}, u32[]{:S(2)}) collective-permute-start(bf16[2,256,384]{2,1,0:T(8,128)(2,1)S(1)} %get-tuple-element.32), channel_id=1, source_target_pairs={{0,12},{1,13},{2,14},{3,15},{4,8},{5,9},{6,10},{7,11},{8,4},{9,5},... | collective-permute-start | bytes 1179656 | tf_op jit(solution)/shard_map/ppermute | solution.py:292
  71.0 5.1 %field_0.1 = (bf16[2,256,384]{2,1,0:T(8,128)(2,1)S(1)}, bf16[2,256,384]{2,1,0:T(8,128)(2,1)S(1)}, bf16[2,256,384]{2,1,0:T(8,128)(2,1)S(1)}, bf16[2,256,384]{2,1,0:T(8,128)(2,1)S(1)}) custom-call(s32[7]{0:T(128)S(1)} %pad_add_fusion.meta, bf16[4,8,8,16,512]{4,3,2,1,0:T(8,128)(2,1)} %resident_slices.1.own_ref, ...), custom_call_target="tpu_custom_call" | custom-call | flops 1610612736 | bytes 5000000 | tf_op jit(solution)/shard_map/field_0/pallas_call | solution.py:183
  78.8 3.8 %collective-permute-done.19 = bf16[2,256,384]{2,1,0:T(8,128)(2,1)S(1)} collective-permute-done((bf16[2,256,384]{2,1,0:T(8,128)(2,1)S(1)}, bf16[2,256,384]{2,1,0:T(8,128)(2,1)S(1)}, u32[]{:S(2)}, u32[]{:S(2)}) %collective-permute-start.19) | collective-permute-done | bytes 393248 | tf_op jit(solution)/shard_map/ppermute | solution.py:292
  83.1 3.7 %collective-permute-done.17 = bf16[2,256,384]{2,1,0:T(8,128)(2,1)S(1)} collective-permute-done((bf16[2,256,384]{2,1,0:T(8,128)(2,1)S(1)}, bf16[2,256,384]{2,1,0:T(8,128)(2,1)S(1)}, u32[]{:S(2)}, u32[]{:S(2)}) %collective-permute-start.17) | collective-permute-done | bytes 393248 | tf_op jit(solution)/shard_map/ppermute | solution.py:292
  87.5 3.6 %collective-permute-done.9 = bf16[2,256,384]{2,1,0:T(8,128)(2,1)S(1)} collective-permute-done((bf16[2,256,384]{2,1,0:T(8,128)(2,1)S(1)}, bf16[2,256,384]{2,1,0:T(8,128)(2,1)S(1)}, u32[]{:S(2)}, u32[]{:S(2)}) %collective-permute-start.9) | collective-permute-done | bytes 393248 | tf_op jit(solution)/shard_map/ppermute | solution.py:292
  91.2 3.0 %collective-permute-done.7 = bf16[2,256,384]{2,1,0:T(8,128)(2,1)S(1)} collective-permute-done((bf16[2,256,384]{2,1,0:T(8,128)(2,1)S(1)}, bf16[2,256,384]{2,1,0:T(8,128)(2,1)S(1)}, u32[]{:S(2)}, u32[]{:S(2)}) %collective-permute-start.7) | collective-permute-done | bytes 393248 | tf_op jit(solution)/shard_map/ppermute | solution.py:292
  94.2 1.7 %collective-permute-start.20 = (bf16[256,384]{1,0:T(8,128)(2,1)S(1)}, bf16[256,384]{1,0:T(8,128)(2,1)S(1)}, u32[]{:S(2)}, u32[]{:S(2)}) collective-permute-start(bf16[256,384]{1,0:T(8,128)(2,1)S(1)} %fusion.3), channel_id=1, source_target_pairs={{0,4},{1,5},{2,6},{3,7},{4,0},{5,1},{6,2},{7,3},{8,12},{9,13},{10,... | collective-permute-start | bytes 589832 | tf_op jit(solution)/shard_map/ppermute | solution.py:292
  96.0 2.5 %collective-permute-done.40 = bf16[256,384]{1,0:T(8,128)(2,1)S(1)} collective-permute-done((bf16[256,384]{1,0:T(8,128)(2,1)S(1)}, bf16[256,384]{1,0:T(8,128)(2,1)S(1)}, u32[]{:S(2)}, u32[]{:S(2)}) %collective-permute-start.40) | collective-permute-done | bytes 196640 | tf_op jit(solution)/shard_map/ppermute | solution.py:292
  98.4 3.3 %collective-permute-start.18 = (bf16[256,384]{1,0:T(8,128)(2,1)S(1)}, bf16[256,384]{1,0:T(8,128)(2,1)S(1)}, u32[]{:S(2)}, u32[]{:S(2)}) collective-permute-start(bf16[256,384]{1,0:T(8,128)(2,1)S(1)} %fusion.2), channel_id=1, source_target_pairs={{0,12},{1,13},{2,14},{3,15},{4,8},{5,9},{6,10},{7,11},{8,4},{9,5},... | collective-permute-start | bytes 589832 | tf_op jit(solution)/shard_map/ppermute | solution.py:292
  102.6 3.3 %collective-permute-start.8 = (bf16[256,384]{1,0:T(8,128)(2,1)S(1)}, bf16[256,384]{1,0:T(8,128)(2,1)S(1)}, u32[]{:S(2)}, u32[]{:S(2)}) collective-permute-start(bf16[256,384]{1,0:T(8,128)(2,1)S(1)} %fusion), channel_id=1, source_target_pairs={{0,12},{1,13},{2,14},{3,15},{4,8},{5,9},{6,10},{7,11},{8,4},{9,5},... | collective-permute-start | bytes 589832 | tf_op jit(solution)/shard_map/ppermute | solution.py:292
  108.6 2.4 %collective-permute-done.10 = bf16[256,384]{1,0:T(8,128)(2,1)S(1)} collective-permute-done((bf16[256,384]{1,0:T(8,128)(2,1)S(1)}, bf16[256,384]{1,0:T(8,128)(2,1)S(1)}, u32[]{:S(2)}, u32[]{:S(2)}) %collective-permute-start.10) | collective-permute-done | bytes 196640 | tf_op jit(solution)/shard_map/ppermute | solution.py:292
  113.0 2.1 %collective-permute-done.21.refs_5_ = bf16[2,128,384]{2,1,0:T(8,128)(2,1)S(1)} collective-permute-done((bf16[2,128,384]{2,1,0:T(8,128)(2,1)S(1)}, bf16[2,128,384]{2,1,0:T(8,128)(2,1)S(1)}, u32[]{:S(2)}, u32[]{:S(2)}) %collective-permute-start.21) | collective-permute-done | bytes 196640 | tf_op jit(solution)/shard_map/ppermute | solution.py:292
  115.1 2.1 %collective-permute-done.11.refs_2_ = bf16[2,128,384]{2,1,0:T(8,128)(2,1)S(1)} collective-permute-done((bf16[2,128,384]{2,1,0:T(8,128)(2,1)S(1)}, bf16[2,128,384]{2,1,0:T(8,128)(2,1)S(1)}, u32[]{:S(2)}, u32[]{:S(2)}) %collective-permute-start.11) | collective-permute-done | bytes 196640 | tf_op jit(solution)/shard_map/ppermute | solution.py:292
  117.2 2.3 %pack.1 = bf16[64,2,16,384]{3,2,1,0:T(8,128)(2,1)} custom-call(s32[64]{0:T(128)S(1)} %select_reduce_fusion.slot_ref, f32[128,384]{1,0:T(8,128)S(1)} %slice.269.refs_0_, f32[128,384]{1,0:T(8,128)S(1)} %slice.272.refs_1_, bf16[2,128,384]{2,1,0:T(8,128)(2,1)S(1)} %collective-permute-done.11.refs_2_, f32[128,384]{1,0:T(8,128)S(1)} %slice.280.refs_3_, ...), custom_call_target="tpu_custom_call" | custom-call | flops 1000000 | bytes 4000000 | tf_op jit(solution)/shard_map/pack/pallas_call | solution.py:223
  119.5 14.1 %all-to-all-start = ((bf16[16,4,2,16,384]{4,3,2,1,0:T(8,128)(2,1)}), bf16[16,4,2,16,384]{4,3,2,1,0:T(8,128)(2,1)S(1)}, u32[]{:S(2)}, u32[]{:S(2)}) async-start(bf16[16,4,2,16,384]{4,3,2,1,0:T(8,128)(2,1)} %bitcast.28), calls=%async_computation | async-start | bytes 3145728 | tf_op jit(solution)/shard_map/all_to_all | solution.py:361
  133.9 21.4 %all-to-all-done.rows_ref = bf16[16,4,2,16,384]{4,3,2,1,0:T(8,128)(2,1)S(1)} async-done(((bf16[16,4,2,16,384]{4,3,2,1,0:T(8,128)(2,1)}), bf16[16,4,2,16,384]{4,3,2,1,0:T(8,128)(2,1)S(1)}, u32[]{:S(2)}, u32[]{:S(2)}) %all-to-all-start) | async-done | bytes 1572896 | tf_op jit(solution)/shard_map/all_to_all | solution.py:361
  155.3 5.3 %contract.1 = bf16[4,2,128,1024]{3,2,1,0:T(8,128)(2,1)} custom-call(s32[4]{0:T(128)S(1)} %and_select_fusion.1.which, s32[4]{0:T(128)S(1)} %get-tuple-element.41.filled, bf16[16,4,2,16,384]{4,3,2,1,0:T(8,128)(2,1)S(1)} %all-to-all-done.rows_ref, bf16[4,8,2,48,1024]{4,3,2,1,0:T(8,128)(2,1)} %bitcast.55), custom_call_target="tpu_custom_call" | custom-call | flops 1600000000 | bytes 10000000 | tf_op jit(solution)/shard_map/contract/pallas_call | solution.py:266
  (139 shorter events, 24.1 us)
Async XLA Ops:
  10.2 37.3 %collective-permute-start = (bf16[4,8,8,16,512]{4,3,2,1,0:T(8,128)(2,1)}, bf16[4,8,8,16,512]{4,3,2,1,0:T(8,128)(2,1)}, u32[]{:S(2)}, u32[]{:S(2)}) collective-permute-start(bf16[4,8,8,16,512]{4,3,2,1,0:T(8,128)(2,1)} %resident_slices.1.own_ref), channel_id=1, source_target_pairs={{0,1},{1,0},{2,3},{3,2},{4,5},{5,4},{6,7},{7,6},{8,9},{9,8},{10,11... | collective-permute-start | bytes 12582920 | tf_op jit(solution)/shard_map/ppermute | solution.py:292
  18.7 6.4 %collective-permute-start.32 = (bf16[2,48,512]{2,1,0:T(8,128)(2,1)S(1)}, bf16[2,48,512]{2,1,0:T(8,128)(2,1)S(1)}, u32[]{:S(2)}, u32[]{:S(2)}) collective-permute-start(bf16[2,48,512]{2,1,0:T(8,128)(2,1)S(1)} %pad_maximum_fusion.18), channel_id=1, source_target_pairs={{0,64},{16,80},{32,96},{48,112},{64,0},{80,16},{96,32},{112,48},{1... | collective-permute-start | bytes 294920 | tf_op jit(solution)/shard_map/ppermute | solution.py:292
  21.9 7.3 %collective-permute-start.12 = (bf16[2,48,512]{2,1,0:T(8,128)(2,1)S(1)}, bf16[2,48,512]{2,1,0:T(8,128)(2,1)S(1)}, u32[]{:S(2)}, u32[]{:S(2)}) collective-permute-start(bf16[2,48,512]{2,1,0:T(8,128)(2,1)S(1)} %pad_maximum_fusion.14), channel_id=1, source_target_pairs={{0,64},{16,80},{32,96},{48,112},{64,0},{80,16},{96,32},{112,48},{1... | collective-permute-start | bytes 294920 | tf_op jit(solution)/shard_map/ppermute | solution.py:292
  25.0 6.7 %collective-permute-start.2 = (bf16[2,48,512]{2,1,0:T(8,128)(2,1)S(1)}, bf16[2,48,512]{2,1,0:T(8,128)(2,1)S(1)}, u32[]{:S(2)}, u32[]{:S(2)}) collective-permute-start(bf16[2,48,512]{2,1,0:T(8,128)(2,1)S(1)} %pad_maximum_fusion.12), channel_id=1, source_target_pairs={{0,64},{16,80},{32,96},{48,112},{64,0},{80,16},{96,32},{112,48},{1... | collective-permute-start | bytes 294920 | tf_op jit(solution)/shard_map/ppermute | solution.py:292
  25.1 7.6 %collective-permute-start.35 = (bf16[2,48,512]{2,1,0:T(8,128)(2,1)S(1)}, bf16[2,48,512]{2,1,0:T(8,128)(2,1)S(1)}, u32[]{:S(2)}, u32[]{:S(2)}) collective-permute-start(bf16[2,48,512]{2,1,0:T(8,128)(2,1)S(1)} %pad_maximum_fusion.23.b0), channel_id=1, source_target_pairs={{0,48},{16,32},{32,16},{48,0},{64,112},{80,96},{96,80},{112,64},{1... | collective-permute-start | bytes 294920 | tf_op jit(solution)/shard_map/ppermute | solution.py:292
  27.7 6.9 %collective-permute-start.33 = (bf16[2,48,512]{2,1,0:T(8,128)(2,1)S(1)}, bf16[2,48,512]{2,1,0:T(8,128)(2,1)S(1)}, u32[]{:S(2)}, u32[]{:S(2)}) collective-permute-start(bf16[2,48,512]{2,1,0:T(8,128)(2,1)S(1)} %pad_maximum_fusion.19.a0), channel_id=1, source_target_pairs={{0,16},{16,0},{32,48},{48,32},{64,80},{80,64},{96,112},{112,96},{1... | collective-permute-start | bytes 294920 | tf_op jit(solution)/shard_map/ppermute | solution.py:292
  39.2 6.2 %collective-permute-start.34 = (bf16[4,48,512]{2,1,0:T(8,128)(2,1)S(1)}, bf16[4,48,512]{2,1,0:T(8,128)(2,1)S(1)}, u32[]{:S(2)}, u32[]{:S(2)}) collective-permute-start(bf16[4,48,512]{2,1,0:T(8,128)(2,1)S(1)} %pad_maximum_fusion.9), channel_id=1, source_target_pairs={{0,48},{16,32},{32,16},{48,0},{64,112},{80,96},{96,80},{112,64},{1... | collective-permute-start | bytes 589832 | tf_op jit(solution)/shard_map/ppermute | solution.py:292
  40.9 11.8 %collective-permute-start.26 = (bf16[4,48,512]{2,1,0:T(8,128)(2,1)S(1)}, bf16[4,48,512]{2,1,0:T(8,128)(2,1)S(1)}, u32[]{:S(2)}, u32[]{:S(2)}) collective-permute-start(bf16[4,48,512]{2,1,0:T(8,128)(2,1)S(1)} %pad_maximum_fusion.7), channel_id=1, source_target_pairs={{0,16},{16,0},{32,48},{48,32},{64,80},{80,64},{96,112},{112,96},{1... | collective-permute-start | bytes 589832 | tf_op jit(solution)/shard_map/ppermute | solution.py:292
  41.7 11.5 %collective-permute-start.24 = (bf16[4,48,512]{2,1,0:T(8,128)(2,1)S(1)}, bf16[4,48,512]{2,1,0:T(8,128)(2,1)S(1)}, u32[]{:S(2)}, u32[]{:S(2)}) collective-permute-start(bf16[4,48,512]{2,1,0:T(8,128)(2,1)S(1)} %pad_maximum_fusion.6), channel_id=1, source_target_pairs={{0,48},{16,32},{32,16},{48,0},{64,112},{80,96},{96,80},{112,64},{1... | collective-permute-start | bytes 589832 | tf_op jit(solution)/shard_map/ppermute | solution.py:292
  43.8 18.4 %collective-permute-start.16 = (bf16[4,48,512]{2,1,0:T(8,128)(2,1)S(1)}, bf16[4,48,512]{2,1,0:T(8,128)(2,1)S(1)}, u32[]{:S(2)}, u32[]{:S(2)}) collective-permute-start(bf16[4,48,512]{2,1,0:T(8,128)(2,1)S(1)} %pad_maximum_fusion.4), channel_id=1, source_target_pairs={{0,16},{16,0},{32,48},{48,32},{64,80},{80,64},{96,112},{112,96},{1... | collective-permute-start | bytes 589832 | tf_op jit(solution)/shard_map/ppermute | solution.py:292
  45.4 16.9 %collective-permute-start.14 = (bf16[4,48,512]{2,1,0:T(8,128)(2,1)S(1)}, bf16[4,48,512]{2,1,0:T(8,128)(2,1)S(1)}, u32[]{:S(2)}, u32[]{:S(2)}) collective-permute-start(bf16[4,48,512]{2,1,0:T(8,128)(2,1)S(1)} %pad_maximum_fusion.3), channel_id=1, source_target_pairs={{0,48},{16,32},{32,16},{48,0},{64,112},{80,96},{96,80},{112,64},{1... | collective-permute-start | bytes 589832 | tf_op jit(solution)/shard_map/ppermute | solution.py:292
  47.5 19.9 %collective-permute-start.6 = (bf16[4,48,512]{2,1,0:T(8,128)(2,1)S(1)}, bf16[4,48,512]{2,1,0:T(8,128)(2,1)S(1)}, u32[]{:S(2)}, u32[]{:S(2)}) collective-permute-start(bf16[4,48,512]{2,1,0:T(8,128)(2,1)S(1)} %pad_maximum_fusion.1), channel_id=1, source_target_pairs={{0,16},{16,0},{32,48},{48,32},{64,80},{80,64},{96,112},{112,96},{1... | collective-permute-start | bytes 589832 | tf_op jit(solution)/shard_map/ppermute | solution.py:292
  52.7 16.2 %collective-permute-start.4 = (bf16[4,48,512]{2,1,0:T(8,128)(2,1)S(1)}, bf16[4,48,512]{2,1,0:T(8,128)(2,1)S(1)}, u32[]{:S(2)}, u32[]{:S(2)}) collective-permute-start(bf16[4,48,512]{2,1,0:T(8,128)(2,1)S(1)} %pad_maximum_fusion), channel_id=1, source_target_pairs={{0,48},{16,32},{32,16},{48,0},{64,112},{80,96},{96,80},{112,64},{1... | collective-permute-start | bytes 589832 | tf_op jit(solution)/shard_map/ppermute | solution.py:292
  53.3 22.8 %collective-permute-start.39 = (bf16[2,256,384]{2,1,0:T(8,128)(2,1)S(1)}, bf16[2,256,384]{2,1,0:T(8,128)(2,1)S(1)}, u32[]{:S(2)}, u32[]{:S(2)}) collective-permute-start(bf16[2,256,384]{2,1,0:T(8,128)(2,1)S(1)} %get-tuple-element.40), channel_id=1, source_target_pairs={{0,12},{1,13},{2,14},{3,15},{4,8},{5,9},{6,10},{7,11},{8,4},{9,5},... | collective-permute-start | bytes 1179656 | tf_op jit(solution)/shard_map/ppermute | solution.py:292
  62.1 14.2 %collective-permute-start.37 = (bf16[2,256,384]{2,1,0:T(8,128)(2,1)S(1)}, bf16[2,256,384]{2,1,0:T(8,128)(2,1)S(1)}, u32[]{:S(2)}, u32[]{:S(2)}) collective-permute-start(bf16[2,256,384]{2,1,0:T(8,128)(2,1)S(1)} %get-tuple-element.38), channel_id=1, source_target_pairs={{0,4},{1,5},{2,6},{3,7},{4,0},{5,1},{6,2},{7,3},{8,12},{9,13},{10,... | collective-permute-start | bytes 1179656 | tf_op jit(solution)/shard_map/ppermute | solution.py:292
  62.2 14.8 %collective-permute-start.29 = (bf16[2,256,384]{2,1,0:T(8,128)(2,1)S(1)}, bf16[2,256,384]{2,1,0:T(8,128)(2,1)S(1)}, u32[]{:S(2)}, u32[]{:S(2)}) collective-permute-start(bf16[2,256,384]{2,1,0:T(8,128)(2,1)S(1)} %get-tuple-element.36), channel_id=1, source_target_pairs={{0,12},{1,13},{2,14},{3,15},{4,8},{5,9},{6,10},{7,11},{8,4},{9,5},... | collective-permute-start | bytes 1179656 | tf_op jit(solution)/shard_map/ppermute | solution.py:292
  67.5 10.5 %collective-permute-start.27 = (bf16[2,256,384]{2,1,0:T(8,128)(2,1)S(1)}, bf16[2,256,384]{2,1,0:T(8,128)(2,1)S(1)}, u32[]{:S(2)}, u32[]{:S(2)}) collective-permute-start(bf16[2,256,384]{2,1,0:T(8,128)(2,1)S(1)} %get-tuple-element.34), channel_id=1, source_target_pairs={{0,4},{1,5},{2,6},{3,7},{4,0},{5,1},{6,2},{7,3},{8,12},{9,13},{10,... | collective-permute-start | bytes 1179656 | tf_op jit(solution)/shard_map/ppermute | solution.py:292
  68.9 13.8 %collective-permute-start.19 = (bf16[2,256,384]{2,1,0:T(8,128)(2,1)S(1)}, bf16[2,256,384]{2,1,0:T(8,128)(2,1)S(1)}, u32[]{:S(2)}, u32[]{:S(2)}) collective-permute-start(bf16[2,256,384]{2,1,0:T(8,128)(2,1)S(1)} %get-tuple-element.32), channel_id=1, source_target_pairs={{0,12},{1,13},{2,14},{3,15},{4,8},{5,9},{6,10},{7,11},{8,4},{9,5},... | collective-permute-start | bytes 1179656 | tf_op jit(solution)/shard_map/ppermute | solution.py:292
  76.1 10.7 %collective-permute-start.17 = (bf16[2,256,384]{2,1,0:T(8,128)(2,1)S(1)}, bf16[2,256,384]{2,1,0:T(8,128)(2,1)S(1)}, u32[]{:S(2)}, u32[]{:S(2)}) collective-permute-start(bf16[2,256,384]{2,1,0:T(8,128)(2,1)S(1)} %get-tuple-element.30), channel_id=1, source_target_pairs={{0,4},{1,5},{2,6},{3,7},{4,0},{5,1},{6,2},{7,3},{8,12},{9,13},{10,... | collective-permute-start | bytes 1179656 | tf_op jit(solution)/shard_map/ppermute | solution.py:292
  76.3 14.8 %collective-permute-start.9 = (bf16[2,256,384]{2,1,0:T(8,128)(2,1)S(1)}, bf16[2,256,384]{2,1,0:T(8,128)(2,1)S(1)}, u32[]{:S(2)}, u32[]{:S(2)}) collective-permute-start(bf16[2,256,384]{2,1,0:T(8,128)(2,1)S(1)} %get-tuple-element.28), channel_id=1, source_target_pairs={{0,12},{1,13},{2,14},{3,15},{4,8},{5,9},{6,10},{7,11},{8,4},{9,5},... | collective-permute-start | bytes 1179656 | tf_op jit(solution)/shard_map/ppermute | solution.py:292
  77.1 17.1 %collective-permute-start.7 = (bf16[2,256,384]{2,1,0:T(8,128)(2,1)S(1)}, bf16[2,256,384]{2,1,0:T(8,128)(2,1)S(1)}, u32[]{:S(2)}, u32[]{:S(2)}) collective-permute-start(bf16[2,256,384]{2,1,0:T(8,128)(2,1)S(1)} %get-tuple-element.26), channel_id=1, source_target_pairs={{0,4},{1,5},{2,6},{3,7},{4,0},{5,1},{6,2},{7,3},{8,12},{9,13},{10,... | collective-permute-start | bytes 1179656 | tf_op jit(solution)/shard_map/ppermute | solution.py:292
  78.0 20.4 %collective-permute-start.40 = (bf16[256,384]{1,0:T(8,128)(2,1)S(1)}, bf16[256,384]{1,0:T(8,128)(2,1)S(1)}, u32[]{:S(2)}, u32[]{:S(2)}) collective-permute-start(bf16[256,384]{1,0:T(8,128)(2,1)S(1)} %fusion.7), channel_id=1, source_target_pairs={{0,4},{1,5},{2,6},{3,7},{4,0},{5,1},{6,2},{7,3},{8,12},{9,13},{10,... | collective-permute-start | bytes 589832 | tf_op jit(solution)/shard_map/ppermute | solution.py:292
  82.7 19.1 %collective-permute-start.38 = (bf16[256,384]{1,0:T(8,128)(2,1)S(1)}, bf16[256,384]{1,0:T(8,128)(2,1)S(1)}, u32[]{:S(2)}, u32[]{:S(2)}) collective-permute-start(bf16[256,384]{1,0:T(8,128)(2,1)S(1)} %fusion.6), channel_id=1, source_target_pairs={{0,12},{1,13},{2,14},{3,15},{4,8},{5,9},{6,10},{7,11},{8,4},{9,5},... | collective-permute-start | bytes 589832 | tf_op jit(solution)/shard_map/ppermute | solution.py:292
  86.8 15.8 %collective-permute-start.30 = (bf16[256,384]{1,0:T(8,128)(2,1)S(1)}, bf16[256,384]{1,0:T(8,128)(2,1)S(1)}, u32[]{:S(2)}, u32[]{:S(2)}) collective-permute-start(bf16[256,384]{1,0:T(8,128)(2,1)S(1)} %fusion.5), channel_id=1, source_target_pairs={{0,4},{1,5},{2,6},{3,7},{4,0},{5,1},{6,2},{7,3},{8,12},{9,13},{10,... | collective-permute-start | bytes 589832 | tf_op jit(solution)/shard_map/ppermute | solution.py:292
  91.1 14.9 %collective-permute-start.28 = (bf16[256,384]{1,0:T(8,128)(2,1)S(1)}, bf16[256,384]{1,0:T(8,128)(2,1)S(1)}, u32[]{:S(2)}, u32[]{:S(2)}) collective-permute-start(bf16[256,384]{1,0:T(8,128)(2,1)S(1)} %fusion.4), channel_id=1, source_target_pairs={{0,12},{1,13},{2,14},{3,15},{4,8},{5,9},{6,10},{7,11},{8,4},{9,5},... | collective-permute-start | bytes 589832 | tf_op jit(solution)/shard_map/ppermute | solution.py:292
  94.2 12.6 %collective-permute-start.20 = (bf16[256,384]{1,0:T(8,128)(2,1)S(1)}, bf16[256,384]{1,0:T(8,128)(2,1)S(1)}, u32[]{:S(2)}, u32[]{:S(2)}) collective-permute-start(bf16[256,384]{1,0:T(8,128)(2,1)S(1)} %fusion.3), channel_id=1, source_target_pairs={{0,4},{1,5},{2,6},{3,7},{4,0},{5,1},{6,2},{7,3},{8,12},{9,13},{10,... | collective-permute-start | bytes 589832 | tf_op jit(solution)/shard_map/ppermute | solution.py:292
  98.4 9.5 %collective-permute-start.18 = (bf16[256,384]{1,0:T(8,128)(2,1)S(1)}, bf16[256,384]{1,0:T(8,128)(2,1)S(1)}, u32[]{:S(2)}, u32[]{:S(2)}) collective-permute-start(bf16[256,384]{1,0:T(8,128)(2,1)S(1)} %fusion.2), channel_id=1, source_target_pairs={{0,12},{1,13},{2,14},{3,15},{4,8},{5,9},{6,10},{7,11},{8,4},{9,5},... | collective-permute-start | bytes 589832 | tf_op jit(solution)/shard_map/ppermute | solution.py:292
  101.8 9.2 %collective-permute-start.10 = (bf16[256,384]{1,0:T(8,128)(2,1)S(1)}, bf16[256,384]{1,0:T(8,128)(2,1)S(1)}, u32[]{:S(2)}, u32[]{:S(2)}) collective-permute-start(bf16[256,384]{1,0:T(8,128)(2,1)S(1)} %fusion.1), channel_id=1, source_target_pairs={{0,4},{1,5},{2,6},{3,7},{4,0},{5,1},{6,2},{7,3},{8,12},{9,13},{10,... | collective-permute-start | bytes 589832 | tf_op jit(solution)/shard_map/ppermute | solution.py:292
  102.6 8.5 %collective-permute-start.8 = (bf16[256,384]{1,0:T(8,128)(2,1)S(1)}, bf16[256,384]{1,0:T(8,128)(2,1)S(1)}, u32[]{:S(2)}, u32[]{:S(2)}) collective-permute-start(bf16[256,384]{1,0:T(8,128)(2,1)S(1)} %fusion), channel_id=1, source_target_pairs={{0,12},{1,13},{2,14},{3,15},{4,8},{5,9},{6,10},{7,11},{8,4},{9,5},... | collective-permute-start | bytes 589832 | tf_op jit(solution)/shard_map/ppermute | solution.py:292
  106.8 6.2 %collective-permute-start.31 = (bf16[2,128,384]{2,1,0:T(8,128)(2,1)S(1)}, bf16[2,128,384]{2,1,0:T(8,128)(2,1)S(1)}, u32[]{:S(2)}, u32[]{:S(2)}) collective-permute-start(bf16[2,128,384]{2,1,0:T(8,128)(2,1)S(1)} %pad_maximum_fusion.8), channel_id=1, source_target_pairs={{0,2},{1,3},{2,0},{3,1},{4,6},{5,7},{6,4},{7,5},{8,10},{9,11},{10,... | collective-permute-start | bytes 589832 | tf_op jit(solution)/shard_map/ppermute | solution.py:292
  108.0 7.1 %collective-permute-start.21 = (bf16[2,128,384]{2,1,0:T(8,128)(2,1)S(1)}, bf16[2,128,384]{2,1,0:T(8,128)(2,1)S(1)}, u32[]{:S(2)}, u32[]{:S(2)}) collective-permute-start(bf16[2,128,384]{2,1,0:T(8,128)(2,1)S(1)} %pad_maximum_fusion.5), channel_id=1, source_target_pairs={{0,2},{1,3},{2,0},{3,1},{4,6},{5,7},{6,4},{7,5},{8,10},{9,11},{10,... | collective-permute-start | bytes 589832 | tf_op jit(solution)/shard_map/ppermute | solution.py:292
  119.5 35.7 %all-to-all-start = ((bf16[16,4,2,16,384]{4,3,2,1,0:T(8,128)(2,1)}), bf16[16,4,2,16,384]{4,3,2,1,0:T(8,128)(2,1)S(1)}, u32[]{:S(2)}, u32[]{:S(2)}) async-start(bf16[16,4,2,16,384]{4,3,2,1,0:T(8,128)(2,1)} %bitcast.28), calls=%async_computation | async-start | bytes 3145728 | tf_op jit(solution)/shard_map/all_to_all | solution.py:361
  (14 other events, 95.1 us)

commit v2 on v1

v2 whole, which is shorter than its diff:
```python
import functools
import math

import jax
import jax.numpy as jnp
from jax import lax
from jax.experimental import pallas as pl
from jax.experimental.pallas import tpu as pltpu
from jax.sharding import PartitionSpec as P

STRIP = 128
LX = 96
CAP = 4
BF = jnp.bfloat16
F32 = jnp.float32
VMEM_LIMIT = 48 * 1024 * 1024


def phase_pair(diag_mom, start, count):
    lattice_positions = (start + jnp.arange(count, dtype=jnp.int32)) % LX
    turns = diag_mom[:, None] * lattice_positions[None, :] % LX
    angle = 2.0 * math.pi / LX * turns.astype(F32)
    return jnp.cos(angle), jnp.sin(angle)


def params():
    return pltpu.CompilerParams(vmem_limit_bytes=VMEM_LIMIT)


def cost(flops, size):
    return pl.CostEstimate(flops=flops, bytes_accessed=size, transcendentals=0)


LANES = 128


def widen(ref, wide):
    parts, rows, times, _ = ref.shape
    for p in range(parts):
        for h in range(wide.shape[1]):
            x = ref[p, :, :, h * LANES : (h + 1) * LANES]
            wide[p, h] = x.astype(F32).reshape(rows * times, LANES)


def narrow(wide, p, rows):
    return jnp.concatenate([wide[p, h, rows, :] for h in range(wide.shape[1])], axis=1)


def source_kernel(ds, meta, cos_ref, sin_ref, src_ref, after_ref, keep_ref, send_ref, wide):
    _, modes, times, sites = src_ref.shape
    half = modes // 2
    widen(src_ref, wide)
    core = meta[5]
    for n, d in enumerate(ds):
        c = cos_ref[d : d + 1, :]
        s = sin_ref[d : d + 1, :]
        for ref, who in ((keep_ref, core), (send_ref, 1 - core)):
            rows = pl.ds(who * (half * times) + meta[d], half, stride=times)
            re = narrow(wide, 0, rows)
            im = narrow(wide, 1, rows)
            ref[n, :, 0:sites] = (re * c + im * s).astype(BF)
            ref[n, :, sites : 2 * sites] = (im * c - re * s).astype(BF)


def source_slices(ds, meta, cosine, sine, source, after):
    parts, modes, times, sites = source.shape
    piece = jax.ShapeDtypeStruct((len(ds), modes // 2, parts * sites), BF)
    return pl.pallas_call(
        functools.partial(source_kernel, ds),
        out_shape=(piece, piece),
        in_specs=[pl.BlockSpec(memory_space=pltpu.SMEM)]
        + [pl.BlockSpec(memory_space=pltpu.VMEM)] * 3
        + [pl.BlockSpec(memory_space=pl.ANY)],
        out_specs=[pl.BlockSpec(memory_space=pltpu.VMEM)] * 2,
        scratch_shapes=[pltpu.VMEM((parts, sites // LANES, modes * times, LANES), F32)],
        compiler_params=params(),
        cost_estimate=cost(10**6, 2 * 10**6),
        name="source_slices",
    )(meta, cosine, sine, source, after)


def resident_kernel(chunks, meta, res_ref, after_ref, *refs):
    outs, wide = refs[:-1], refs[-1]
    parts, strip, times, sites = res_ref.shape
    rows = outs[0].shape[3]
    groups = strip // rows
    z, y = meta[4], meta[7]
    widen(res_ref, wide)
    for out_ref, n, d in [(r, n, d) for r, ds in zip(outs, chunks) for n, d in enumerate(ds)]:
        for p in range(parts):
            x = narrow(wide, p, pl.ds(meta[d], strip, stride=times)).astype(BF)
            for g in range(groups):
                at = ((g % 2) ^ y) * (groups // 2) + ((g // 2) ^ z)
                out_ref[n, at, 0, :, p * sites : (p + 1) * sites] = x[
                    g * rows : (g + 1) * rows
                ]


def resident_slices(chunks, meta, resident, after, groups):
    parts, res_dev, times, sites = resident.shape
    blocks = res_dev // STRIP
    rows = STRIP // groups
    shapes = [(len(ds), groups, blocks, rows, parts * sites) for ds in chunks]
    return pl.pallas_call(
        functools.partial(resident_kernel, chunks),
        out_shape=[jax.ShapeDtypeStruct(shape, BF) for shape in shapes],
        grid_spec=pltpu.PrefetchScalarGridSpec(
            num_scalar_prefetch=1,
            grid=(blocks,),
            in_specs=[
                pl.BlockSpec((parts, STRIP, times, sites), lambda b, meta: (0, b, 0, 0)),
                pl.BlockSpec(memory_space=pl.ANY),
            ],
            out_specs=[
                pl.BlockSpec((*shape[:2], 1, *shape[3:]), lambda b, meta: (0, 0, b, 0, 0))
                for shape in shapes
            ],
            scratch_shapes=[pltpu.VMEM((parts, sites // LANES, STRIP * times, LANES), F32)],
        ),
        compiler_params=params(),
        cost_estimate=cost(30 * 10**9, 13 * 10**6),
        name="resident_slices",
    )(meta, resident, after)


PLACES = (
    ((0, 4), (1, 5), (3, 7, 2, 6)),
    ((0, 4), (3, 7), (1, 5, 2, 6)),
)


def field_kernel(meta, own_ref, par_ref, a0, a1, a2, b0, b1, b2, after_a, after_b,
                 a_keep, a_send, b_keep, b_send, real_rhs, imag_rhs):
    me = meta[6]
    _, groups, blocks, rows, width = own_ref.shape
    sites = width // 2
    columns = real_rhs.shape[1] * real_rhs.shape[2]
    for side, arrays in enumerate(((a0, a1, a2), (b0, b1, b2))):
        for ref, places in zip(arrays, PLACES[side]):
            for n, place in enumerate(places):
                at = me ^ place
                v = ref[n, 0]
                real_rhs[side, at] = v
                imag_rhs[side, at, :, 0:sites] = v[:, sites:]
                imag_rhs[side, at, :, sites:] = -v[:, 0:sites]

    zs = groups // 2
    tall = blocks * rows
    for k in range(2):
        left = [x[0, k * zs : (k + 1) * zs].reshape(zs * tall, width) for x in (own_ref, par_ref)]

        def product(rhs, left=left):
            total = None
            for n, x in enumerate(left):
                term = lax.dot_general(
                    x,
                    rhs[n].reshape(columns, width),
                    (((1,), (1,)), ((), ())),
                    preferred_element_type=F32,
                )
                total = term if total is None else total + term
            return total.astype(BF).reshape(zs, tall, columns)

        real = product(real_rhs)
        imag = product(imag_rhs)
        a_keep[0, 0, k] = real[0]
        a_send[0, 0, k] = real[1]
        a_send[1, 0, k] = real[2]
        a_keep[1, 0, k] = real[3]
        b_keep[0, 0, k] = imag[0]
        b_keep[1, 0, k] = imag[1]
        b_send[1, 0, k] = imag[2]
        b_send[0, 0, k] = imag[3]


def partial_field(n, at, meta, own, par, side_a, side_b, after_a, after_b):
    _, groups, blocks, rows, width = own.shape
    modes = side_a[0].shape[2]
    columns = 8 * modes
    out = jax.ShapeDtypeStruct((2, n, 2, blocks * rows, columns), BF)
    left = pl.BlockSpec(
        (1, groups, blocks, rows, width), lambda i, meta: (at + i, 0, 0, 0, 0)
    )

    def piece(x):
        return pl.BlockSpec((x.shape[0], 1, modes, width), lambda i, meta: (0, i, 0, 0))

    return pl.pallas_call(
        field_kernel,
        out_shape=(out,) * 4,
        grid_spec=pltpu.PrefetchScalarGridSpec(
            num_scalar_prefetch=1,
            grid=(n,),
            in_specs=[left, left]
            + [piece(x) for x in (*side_a, *side_b)]
            + [pl.BlockSpec(memory_space=pl.ANY)] * 2,
            out_specs=[
                pl.BlockSpec((2, 1, *out.shape[2:]), lambda i, meta: (0, i, 0, 0, 0))
            ]
            * 4,
            scratch_shapes=[pltpu.VMEM((2, 8, modes, width), BF)] * 2,
        ),
        compiler_params=params(),
        cost_estimate=cost(n * 2 * 1024 * 1024 * 768, n * 5 * 10**6),
        name="field",
    )(meta, own, par, *side_a, *side_b, after_a, after_b)


def pack_kernel(counts, slot_ref, *refs):
    ins, out_ref, strips = list(refs[:-2]), refs[-2], refs[-1]
    rows, columns = strips.shape[2:]
    at = 0
    for n, size in counts:
        sums = [ins.pop(0) for _ in range(2)]
        other = ins.pop(0) if size == 3 else None
        blocks = sums[0].shape[1] // rows
        for d in range(n):
            for p in range(2):
                total = sums[p][d]
                if other is not None:
                    total = total + other[p, d].astype(F32)
                strips[at : at + blocks, p] = total.astype(BF).reshape(
                    blocks, rows, columns
                )
            at += blocks

    def one(slot, carry):
        out_ref[slot] = strips[slot_ref[slot]]
        return carry

    lax.fori_loop(0, out_ref.shape[0], one, 0)


def pack(slot_strip, finished, strip_count, rows):
    columns = finished[0][0].shape[-1]
    flat = [x for group in finished for x in group]
    counts = [(group[0].shape[0], len(group)) for group in finished]
    return pl.pallas_call(
        functools.partial(pack_kernel, counts),
        out_shape=jax.ShapeDtypeStruct((slot_strip.shape[0], 2, rows, columns), BF),
        in_specs=[pl.BlockSpec(memory_space=pltpu.SMEM)]
        + [pl.BlockSpec(memory_space=pltpu.VMEM)] * len(flat),
        out_specs=pl.BlockSpec(memory_space=pltpu.VMEM),
        scratch_shapes=[pltpu.VMEM((strip_count, 2, rows, columns), BF)],
        compiler_params=params(),
        cost_estimate=cost(10**6, 4 * 10**6),
        name="pack",
    )(slot_strip, *flat)


def insertion_kernel(which, filled, rows_ref, ins_ref, out_ref):
    t = pl.program_id(0)
    columns = rows_ref.shape[-1]
    groups = rows_ref.shape[0] // 2
    width = ins_ref.shape[-1]

    @pl.when(filled[t] == 0)
    def _():
        out_ref[...] = jnp.zeros_like(out_ref)

    @pl.when(filled[t] != 0)
    def _():
        total = None
        for core in range(2):
            lhs = jnp.concatenate(
                [rows_ref[2 * g + core, 0, p] for p in range(2) for g in range(groups)],
                axis=0,
            )
            rhs = ins_ref[0, :, core].reshape(columns, width)
            term = jnp.dot(lhs, rhs, preferred_element_type=F32)
            total = term if total is None else total + term
        out_ref[0] = total.astype(BF).reshape(2, STRIP, width)


def contract(which, filled, received, insertion):
    senders, cap, parts, rows, columns = received.shape
    diagrams, _, width = insertion.shape
    n_mode = 8
    modes = columns // n_mode
    split = insertion.reshape(diagrams, n_mode, 2, modes, width)
    return pl.pallas_call(
        insertion_kernel,
        out_shape=jax.ShapeDtypeStruct((cap, parts, STRIP, width), BF),
        grid_spec=pltpu.PrefetchScalarGridSpec(
            num_scalar_prefetch=2,
            grid=(cap,),
            in_specs=[
                pl.BlockSpec(
                    (senders, 1, parts, rows, columns), lambda t, w, f: (0, t, 0, 0, 0)
                ),
                pl.BlockSpec(
                    (1, n_mode, 2, modes, width), lambda t, w, f: (w[t], 0, 0, 0, 0)
                ),
            ],
            out_specs=pl.BlockSpec(
                (1, parts, STRIP, width), lambda t, w, f: (t, 0, 0, 0)
            ),
        ),
        compiler_params=params(),
        cost_estimate=cost(16 * 10**8, 10**7),
        name="contract",
    )(which, filled, received, split)


def swap(x, axis, bits):
    n = lax.axis_size(axis)
    return lax.ppermute(x, axis, [(i, i ^ bits) for i in range(n)])


def swap_both(x):
    n_mode, n_space = lax.axis_size("mode"), lax.axis_size("space")
    bits = YHI * n_space + CORE
    pairs = [(i, i ^ bits) for i in range(n_mode * n_space)]
    return lax.ppermute(x, ("mode", "space"), pairs)


CHUNKS = ((0, 1), (2, 3))
WAIT = (None, 1)

Z1, Z3, Y1, CORE = 4, 12, 2, 1
X1, X3, YHI = 1, 3, 4


def slots(owner_list, n_space, me_space):
    strip_count = owner_list.shape[0]
    same = owner_list[:, None] == owner_list[None, :]
    order = jnp.arange(strip_count, dtype=jnp.int32)
    earlier = order[None, :] < order[:, None]
    rank = jnp.sum((same & earlier).astype(jnp.int32), axis=1)
    slot = owner_list * CAP + rank
    numbers = jnp.arange(n_space * CAP, dtype=jnp.int32)
    match = slot[None, :] == numbers[:, None]
    slot_strip = jnp.sum(jnp.where(match, order[None, :], 0), axis=1)
    mine = me_space * CAP + jnp.arange(CAP, dtype=jnp.int32)
    my_match = slot[None, :] == mine[:, None]
    my_strip = jnp.sum(jnp.where(my_match, order[None, :], 0), axis=1)
    filled = jnp.sum(my_match.astype(jnp.int32), axis=1)
    return slot_strip, my_strip, filled


def gather(a0, b0):
    a1 = swap(a0, "mode", X1)
    b1 = swap(b0, "mode", X3)
    a2 = swap(jnp.concatenate([a0, a1]), "mode", X3)
    b2 = swap(jnp.concatenate([b0, b1]), "mode", X1)
    return (a0, a1, a2), (b0, b1, b2)


def sum_z(a_keep, a_send, b_keep, b_send):
    a_in = swap(a_send, "space", Z1)
    b_in = swap(b_send, "space", Z3)
    a_pass = (a_keep[1].astype(F32) + a_in[1].astype(F32)).astype(BF)
    b_pass = (b_keep[1].astype(F32) + b_in[1].astype(F32)).astype(BF)
    a_last = swap(a_pass, "space", Z3)
    b_last = swap(b_pass, "space", Z1)
    a_sum = a_keep[0].astype(F32) + a_in[0].astype(F32) + a_last.astype(F32)
    b_sum = b_keep[0].astype(F32) + b_in[0].astype(F32) + b_last.astype(F32)
    return a_sum, b_sum, (a_in, b_in)


def on_device(resident, source, insertion, owners, diag_time, diag_mom):
    slab = resident.shape[3]
    n_space = lax.axis_size("space")
    diagrams = insertion.shape[0]
    blocks = resident.shape[1] // STRIP
    groups = n_space // 2
    me_space = lax.axis_index("space")
    me_mode = lax.axis_index("mode")
    place = [me_space // 4, me_space % 2, me_mode, me_space // 2 % 2]
    meta = jnp.concatenate([diag_time, jnp.stack(place).astype(jnp.int32)])
    cosine, sine = phase_pair(diag_mom, me_space * slab, slab)

    def first_phase(ds, after):
        keep, send = source_slices(ds, meta, cosine, sine, source, after)
        arrived = swap(send, "space", CORE)
        far_keep = swap(keep, "mode", YHI)
        far_arrived = swap_both(send)
        return (keep, far_keep), (arrived, far_arrived)

    def part(pair, lo, hi):
        return jnp.stack([x[lo:hi] for x in pair])

    slot_strip, my_strip, filled = slots(owners[:, 0], n_space, me_space)
    pairs = first_phase(tuple(range(diagrams)), meta)
    beside = swap(resident, "space", CORE)
    vectors = resident_slices(CHUNKS, meta, resident, pairs[0][0], groups)
    across = resident_slices(CHUNKS, meta, beside, pairs[0][0], groups)

    finished, fields, landed = [], (meta, meta), [(meta, meta)]
    for chunk, (ds, own, par) in enumerate(zip(CHUNKS, vectors, across)):
        sides = gather(*(part(pair, ds[0], ds[-1] + 1) for pair in pairs))
        after = fields[:2] if WAIT[chunk] is None else landed[WAIT[chunk]]
        fields = partial_field(len(ds), 0, meta, own, par, *sides, *after)
        a_sum, b_sum, first = sum_z(*fields)
        landed.append(first)
        over_y = swap(jnp.stack([a_sum[:, 1], b_sum[:, 1]]).astype(BF), "space", Y1)
        finished.append((a_sum[:, 0], b_sum[:, 0], over_y))

    outgoing = pack(slot_strip, finished, diagrams * blocks, STRIP // groups)
    outgoing = outgoing.reshape(n_space, CAP, *outgoing.shape[1:])
    received = lax.all_to_all(outgoing, "space", 0, 0, tiled=True)
    return contract(my_strip // blocks, filled, received, insertion)


def solution(mesh):
    in_specs = (
        P(None, "mode", None, "space"),
        P(None, "mode", None, "space"),
        P(),
        P("mode", None),
        P(),
        P(),
    )
    out_specs = P("space", None, "mode", None)
    return jax.shard_map(
        on_device, mesh=mesh, in_specs=in_specs, out_specs=out_specs, check_vma=False
    )
```

time: 162 us -> 152 us (0.938)
  starting transfers between devices: 60.4 us -> 35 us
  waiting for transfers between devices: 58.2 us -> 66.7 us
  local copies, waits for them, and re-layouts: 0.3 us -> 7.44 us
    ppermute x42 -> x21, starting transfers between devices: 46.3 us -> 20.3 us  [swap(): return lax.ppermute(x, axis, [(i, i ^ bits) for i in range(n)])]
    ppermute x42 -> x21, waiting for transfers between devices: 36.8 us -> 45.4 us  [swap(): return lax.ppermute(x, axis, [(i, i ^ bits) for i in range(n)])]
    pallas_call x3 -> x4, Pallas kernels: 12.6 us -> 19.1 us  [the longest x2 16 us: resident_slices(): pl.pallas_call(functools.partial(resident_kernel, chunks), out_shape=[jax...]
    pallas_call x4 -> x2, Pallas kernels: 20.4 us -> 14.7 us  [partial_field(): pl.pallas_call(field_kernel, out_shape=(out,) * 4, grid_spec=pltpu.Prefet...]
    unnamed x6 -> x12, local copies, waits for them, and re-layouts: 0.01 us -> 5.08 us
    ppermute x0 -> x1, starting transfers between devices: none -> 3.39 us  [swap_both(): return lax.ppermute(x, ('mode', 'space'), pairs)]
    all_to_all x1, starting transfers between devices: 14.1 us -> 11.4 us  [on_device(): received = lax.all_to_all(outgoing, 'space', 0, 0, tiled=True)]
  transfers between devices with their start and end apart: 43 -> 23, of which waited for: 19 -> 9; matrix products, arithmetic and copies ran while one was open for 1% -> 3% of each run, Pallas kernels for 13% -> 16%
where the time goes in v2:
time: 152 us; the launch traced here: 151 us
  waiting for transfers between devices  66.7 us (44%)
  Pallas kernels  38.4 us (25%)
  starting transfers between devices  35 us (23%)
  local copies, waits for them, and re-layouts  7.44 us (5%)
  other arithmetic  2.56 us (2%)
    ppermute x21, waiting for transfers between devices, swap(): return lax.ppermute(x, axis, [(i, i ^ bits) for i in range(n)])  45.4 us
    all_to_all x1, waiting for transfers between devices, on_device(): received = lax.all_to_all(outgoing, 'space', 0, 0, tiled=True)  21.3 us
    ppermute x21, starting transfers between devices, swap(): return lax.ppermute(x, axis, [(i, i ^ bits) for i in range(n)])  20.3 us
    pallas_call x2, Pallas kernels, resident_slices(): pl.pallas_call(functools.partial(resident_kernel, chunks), out_shape=[jax...  16 us
    pallas_call x2, Pallas kernels, partial_field(): pl.pallas_call(field_kernel, out_shape=(out,) * 4, grid_spec=pltpu.Prefet...  14.7 us
    all_to_all x1, starting transfers between devices, on_device(): received = lax.all_to_all(outgoing, 'space', 0, 0, tiled=True)  11.4 us
    unnamed x12, local copies, waits for them, and re-layouts  5.08 us
    pallas_call x1, Pallas kernels, contract(): pl.pallas_call(insertion_kernel, out_shape=jax.ShapeDtypeStruct((cap, par...  4.57 us
  transfers between devices with their start and end apart: 23, of which 9 were waited for; matrix products, arithmetic and copies ran while one was open for 3% of the time, Pallas kernels for 16%

profile of v2, /device:TPU:1, one launch (start us, length us, event | category | flops | bytes accessed | tf_op | source)
XLA Modules:
  0.0 150.6 jit_solution(18083516873550799061)
XLA Ops:
  0.0 1.4 collective-permute-start
  3.0 1.1 copy-done
  5.1 3.4 %collective-permute-start.5 = (bf16[4,48,512]{2,1,0:T(8,128)(2,1)S(1)}, bf16[4,48,512]{2,1,0:T(8,128)(2,1)S(1)}, u32[]{:S(2)}, u32[]{:S(2)}) collective-permute-start(bf16[4,48,512]{2,1,0:T(8,128)(2,1)S(1)} %get-tuple-element.22), channel_id=1, source_target_pairs={{0,65},{1,64},{2,67},{3,66},{4,69},{5,68},{6,71},{7,70},{8,73},{9,... | collective-permute-start | bytes 589832 | tf_op jit(solution)/shard_map/ppermute | solution.py:314
  8.5 8.0 %resident_slices.2 = (bf16[2,8,8,16,512]{4,3,2,1,0:T(8,128)(2,1)S(1)}, bf16[2,8,8,16,512]{4,3,2,1,0:T(8,128)(2,1)S(1)}) custom-call(s32[8]{0:T(128)S(1)} %concatenate.19.meta.after_ref.after_a.after_b, bf16[2,1024,8,256]{3,2,1,0:T(8,128)(2,1)} %res_ref.1, bf16[4,48,512]{2,1,0:T(8,128)(2,1)S(1)} %get-tuple-element.19.after_ref), custom_call_target="tpu_custom_call" | custom-call | flops 30000001024 | bytes 13000000 | tf_op jit(solution)/shard_map/resident_slices/pallas_call | solution.py:104
  16.5 1.3 copy-done.3
  17.9 2.6 %collective-permute-start.6 = (bf16[2,2,48,512]{3,2,1,0:T(8,128)(2,1)S(1)}, bf16[2,2,48,512]{3,2,1,0:T(8,128)(2,1)S(1)}, u32[]{:S(2)}, u32[]{:S(2)}) collective-permute-start(bf16[2,2,48,512]{3,2,1,0:T(8,128)(2,1)S(1)} %pad_maximum_fusion.7.b0), channel_id=1, source_target_pairs={{0,48},{16,32},{32,16},{48,0},{64,112},{80,96},{96,80},{112,64},{1... | collective-permute-start | bytes 589832 | tf_op jit(solution)/shard_map/ppermute | solution.py:307
  20.8 4.4 %collective-permute-done.6.b1 = bf16[2,2,48,512]{3,2,1,0:T(8,128)(2,1)S(1)} collective-permute-done((bf16[2,2,48,512]{3,2,1,0:T(8,128)(2,1)S(1)}, bf16[2,2,48,512]{3,2,1,0:T(8,128)(2,1)S(1)}, u32[]{:S(2)}, u32[]{:S(2)}) %collective-permute-start.6) | collective-permute-done | bytes 196640 | tf_op jit(solution)/shard_map/ppermute | solution.py:307
  25.5 1.0 collective-permute-done.2.a1
  26.5 1.6 %collective-permute-start.3 = (bf16[4,2,48,512]{3,2,1,0:T(8,128)(2,1)S(1)}, bf16[4,2,48,512]{3,2,1,0:T(8,128)(2,1)S(1)}, u32[]{:S(2)}, u32[]{:S(2)}) collective-permute-start(bf16[4,2,48,512]{3,2,1,0:T(8,128)(2,1)S(1)} %pad_maximum_fusion), channel_id=1, source_target_pairs={{0,48},{16,32},{32,16},{48,0},{64,112},{80,96},{96,80},{112,64},{1... | collective-permute-start | bytes 1179656 | tf_op jit(solution)/shard_map/ppermute | solution.py:307
  28.1 8.0 %resident_slices.3 = (bf16[2,8,8,16,512]{4,3,2,1,0:T(8,128)(2,1)S(1)}, bf16[2,8,8,16,512]{4,3,2,1,0:T(8,128)(2,1)S(1)}) custom-call(s32[8]{0:T(128)S(1)} %concatenate.19.meta.after_ref.after_a.after_b, bf16[2,1024,8,256]{3,2,1,0:T(8,128)(2,1)} %collective-permute-done.res_ref, bf16[4,48,512]{2,1,0:T(8,128)(2,1)S(1)} %get-tuple-element.19.after_ref), custom_call_target="tpu_custom_call" | custom-call | flops 30000001024 | bytes 13000000 | tf_op jit(solution)/shard_map/resident_slices/pallas_call | solution.py:104
  36.1 1.3 copy-done.2
  37.5 1.3 copy-done.4
  38.8 7.4 %field.2 = (bf16[2,2,2,128,384]{4,3,2,1,0:T(8,128)(2,1)S(1)}, bf16[2,2,2,128,384]{4,3,2,1,0:T(8,128)(2,1)S(1)}, bf16[2,2,2,128,384]{4,3,2,1,0:T(8,128)(2,1)S(1)}, bf16[2,2,2,128,384]{4,3,2,1,0:T(8,128)(2,1)S(1)}) custom-call(s32[8]{0:T(128)S(1)} %concatenate.19.meta.after_ref.after_a.after_b, bf16[2,8,8,16,512]{4,3,2,1,0:T(8,128)(2,1)} %copy-done.3, ...), custom_call_target="tpu_custom_call" | custom-call | flops 3221225472 | bytes 10000000 | tf_op jit(solution)/shard_map/field/pallas_call | solution.py:188
  46.2 3.8 %collective-permute-start.10 = (bf16[2,2,2,128,384]{4,3,1,2,0:T(8,128)(2,1)S(1)}, bf16[2,2,2,128,384]{4,3,1,2,0:T(8,128)(2,1)S(1)}, u32[]{:S(2)}, u32[]{:S(2)}) collective-permute-start(bf16[2,2,2,128,384]{4,3,1,2,0:T(8,128)(2,1)S(1)} %copy.25), channel_id=1, source_target_pairs={{0,12},{1,13},{2,14},{3,15},{4,8},{5,9},{6,10},{7,11},{8,4},{9,5},... | collective-permute-start | bytes 2359304 | tf_op jit(solution)/shard_map/ppermute | solution.py:307
  50.3 1.2 collective-permute-start.15
  51.7 4.7 %collective-permute-done.15.b1 = bf16[2,2,48,512]{3,2,1,0:T(8,128)(2,1)S(1)} collective-permute-done((bf16[2,2,48,512]{3,2,1,0:T(8,128)(2,1)S(1)}, bf16[2,2,48,512]{3,2,1,0:T(8,128)(2,1)S(1)}, u32[]{:S(2)}, u32[]{:S(2)}) %collective-permute-start.15) | collective-permute-done | bytes 196640 | tf_op jit(solution)/shard_map/ppermute | solution.py:307
  56.6 1.5 collective-permute-start.14
  58.1 8.4 %collective-permute-done.10 = bf16[2,2,2,128,384]{4,3,1,2,0:T(8,128)(2,1)S(1)} collective-permute-done((bf16[2,2,2,128,384]{4,3,1,2,0:T(8,128)(2,1)S(1)}, bf16[2,2,2,128,384]{4,3,1,2,0:T(8,128)(2,1)S(1)}, u32[]{:S(2)}, u32[]{:S(2)}) %collective-permute-start.10) | collective-permute-done | bytes 786464 | tf_op jit(solution)/shard_map/ppermute | solution.py:307
  67.6 1.6 %collective-permute-start.9 = (bf16[2,2,128,384]{3,2,0,1:T(8,128)(2,1)S(1)}, bf16[2,2,128,384]{3,2,0,1:T(8,128)(2,1)S(1)}, u32[]{:S(2)}, u32[]{:S(2)}) collective-permute-start(bf16[2,2,128,384]{3,2,0,1:T(8,128)(2,1)S(1)} %fusion), channel_id=1, source_target_pairs={{0,12},{1,13},{2,14},{3,15},{4,8},{5,9},{6,10},{7,11},{8,4},{9,5},... | collective-permute-start | bytes 1179656 | tf_op jit(solution)/shard_map/ppermute | solution.py:307
  69.3 1.0 copy.28.after_b
  70.3 7.4 %field.3 = (bf16[2,2,2,128,384]{4,3,2,1,0:T(8,128)(2,1)S(1)}, bf16[2,2,2,128,384]{4,3,2,1,0:T(8,128)(2,1)S(1)}, bf16[2,2,2,128,384]{4,3,2,1,0:T(8,128)(2,1)S(1)}, bf16[2,2,2,128,384]{4,3,2,1,0:T(8,128)(2,1)S(1)}) custom-call(s32[8]{0:T(128)S(1)} %concatenate.19.meta.after_ref.after_a.after_b, bf16[2,8,8,16,512]{4,3,2,1,0:T(8,128)(2,1)} %copy-done.1, ...), custom_call_target="tpu_custom_call" | custom-call | flops 3221225472 | bytes 10000000 | tf_op jit(solution)/shard_map/field/pallas_call | solution.py:188
  77.7 1.2 collective-permute-start.19
  79.7 1.4 collective-permute-start.12
  81.2 14.2 %collective-permute-done.19 = bf16[2,2,2,128,384]{4,3,1,2,0:T(8,128)(2,1)S(1)} collective-permute-done((bf16[2,2,2,128,384]{4,3,1,2,0:T(8,128)(2,1)S(1)}, bf16[2,2,2,128,384]{4,3,1,2,0:T(8,128)(2,1)S(1)}, u32[]{:S(2)}, u32[]{:S(2)}) %collective-permute-start.19) | collective-permute-done | bytes 786464 | tf_op jit(solution)/shard_map/ppermute | solution.py:307
  95.7 1.4 collective-permute-start.18
  97.1 6.7 %collective-permute-done.20 = bf16[2,2,128,384]{3,2,0,1:T(8,128)(2,1)S(1)} collective-permute-done((bf16[2,2,128,384]{3,2,0,1:T(8,128)(2,1)S(1)}, bf16[2,2,128,384]{3,2,0,1:T(8,128)(2,1)S(1)}, u32[]{:S(2)}, u32[]{:S(2)}) %collective-permute-start.20) | collective-permute-done | bytes 393248 | tf_op jit(solution)/shard_map/ppermute | solution.py:307
  104.2 1.4 collective-permute-start.21
  105.6 5.2 %collective-permute-done.21.refs_5_ = bf16[2,2,128,384]{3,2,1,0:T(8,128)(2,1)S(1)} collective-permute-done((bf16[2,2,128,384]{3,2,1,0:T(8,128)(2,1)S(1)}, bf16[2,2,128,384]{3,2,1,0:T(8,128)(2,1)S(1)}, u32[]{:S(2)}, u32[]{:S(2)}) %collective-permute-start.21) | collective-permute-done | bytes 393248 | tf_op jit(solution)/shard_map/ppermute | solution.py:307
  110.9 2.3 %pack.1 = bf16[64,2,16,384]{3,2,1,0:T(8,128)(2,1)} custom-call(s32[64]{0:T(128)S(1)} %select_reduce_fusion.slot_ref, f32[2,128,384]{2,1,0:T(8,128)S(1)} %slice_bitcast_fusion.3.refs_0_, f32[2,128,384]{2,1,0:T(8,128)S(1)} %slice_bitcast_fusion.2.refs_1_, bf16[2,2,128,384]{3,2,1,0:T(8,128)(2,1)S(1)} %collective-permute-done.12.refs_2_, ...), custom_call_target="tpu_custom_call" | custom-call | flops 1000000 | bytes 4000000 | tf_op jit(solution)/shard_map/pack/pallas_call | solution.py:238
  113.2 11.4 %all-to-all-start = ((bf16[16,4,2,16,384]{4,3,2,1,0:T(8,128)(2,1)}), bf16[16,4,2,16,384]{4,3,2,1,0:T(8,128)(2,1)S(1)}, u32[]{:S(2)}, u32[]{:S(2)}) async-start(bf16[16,4,2,16,384]{4,3,2,1,0:T(8,128)(2,1)} %bitcast.29), calls=%async_computation | async-start | bytes 3145728 | tf_op jit(solution)/shard_map/all_to_all | solution.py:401
  124.7 21.3 %all-to-all-done.rows_ref = bf16[16,4,2,16,384]{4,3,2,1,0:T(8,128)(2,1)S(1)} async-done(((bf16[16,4,2,16,384]{4,3,2,1,0:T(8,128)(2,1)}), bf16[16,4,2,16,384]{4,3,2,1,0:T(8,128)(2,1)S(1)}, u32[]{:S(2)}, u32[]{:S(2)}) %all-to-all-start) | async-done | bytes 1572896 | tf_op jit(solution)/shard_map/all_to_all | solution.py:401
  146.0 4.6 %contract.1 = bf16[4,2,128,1024]{3,2,1,0:T(8,128)(2,1)} custom-call(s32[4]{0:T(128)S(1)} %and_select_fusion.1.which, s32[4]{0:T(128)S(1)} %get-tuple-element.33.filled, bf16[16,4,2,16,384]{4,3,2,1,0:T(8,128)(2,1)S(1)} %all-to-all-done.rows_ref, bf16[4,8,2,48,1024]{4,3,2,1,0:T(8,128)(2,1)} %bitcast.56), custom_call_target="tpu_custom_call" | custom-call | flops 1600000000 | bytes 10000000 | tf_op jit(solution)/shard_map/contract/pallas_call | solution.py:281
  (78 shorter events, 6.8 us)
Async XLA Ops:
  0.0 28.1 %collective-permute-start = (bf16[2,1024,8,256]{3,2,1,0:T(8,128)(2,1)}, bf16[2,1024,8,256]{3,2,1,0:T(8,128)(2,1)}, u32[]{:S(2)}, u32[]{:S(2)}) collective-permute-start(bf16[2,1024,8,256]{3,2,1,0:T(8,128)(2,1)} %res_ref.1), channel_id=1, source_target_pairs={{0,1},{1,0},{2,3},{3,2},{4,5},{5,4},{6,7},{7,6},{8,9},{9,8},{10,11... | collective-permute-start | bytes 25165832 | tf_op jit(solution)/shard_map/ppermute | solution.py:307
  3.0 1.1 copy-start
  5.0 12.8 %collective-permute-start.4 = (bf16[4,48,512]{2,1,0:T(8,128)(2,1)S(1)}, bf16[4,48,512]{2,1,0:T(8,128)(2,1)S(1)}, u32[]{:S(2)}, u32[]{:S(2)}) collective-permute-start(bf16[4,48,512]{2,1,0:T(8,128)(2,1)S(1)} %get-tuple-element.22), channel_id=1, source_target_pairs={{0,1},{1,0},{2,3},{3,2},{4,5},{5,4},{6,7},{7,6},{8,9},{9,8},{10,11... | collective-permute-start | bytes 589832 | tf_op jit(solution)/shard_map/ppermute | solution.py:307
  5.1 12.8 %collective-permute-start.5 = (bf16[4,48,512]{2,1,0:T(8,128)(2,1)S(1)}, bf16[4,48,512]{2,1,0:T(8,128)(2,1)S(1)}, u32[]{:S(2)}, u32[]{:S(2)}) collective-permute-start(bf16[4,48,512]{2,1,0:T(8,128)(2,1)S(1)} %get-tuple-element.22), channel_id=1, source_target_pairs={{0,65},{1,64},{2,67},{3,66},{4,69},{5,68},{6,71},{7,70},{8,73},{9,... | collective-permute-start | bytes 589832 | tf_op jit(solution)/shard_map/ppermute | solution.py:314
  8.5 12.1 %collective-permute-start.1 = (bf16[4,48,512]{2,1,0:T(8,128)(2,1)S(1)}, bf16[4,48,512]{2,1,0:T(8,128)(2,1)S(1)}, u32[]{:S(2)}, u32[]{:S(2)}) collective-permute-start(bf16[4,48,512]{2,1,0:T(8,128)(2,1)S(1)} %get-tuple-element.19.after_ref), channel_id=1, source_target_pairs={{0,64},{16,80},{32,96},{48,112},{64,0},{80,16},{96,32},{112,48},{1... | collective-permute-start | bytes 589832 | tf_op jit(solution)/shard_map/ppermute | solution.py:307
  16.5 1.3 copy-start.3
  17.8 8.7 %copy-start.1 = (bf16[2,8,8,16,512]{4,3,2,1,0:T(8,128)(2,1)}, bf16[2,8,8,16,512]{4,3,2,1,0:T(8,128)(2,1)S(1)}, u32[]{:S(2)}) copy-start(bf16[2,8,8,16,512]{4,3,2,1,0:T(8,128)(2,1)S(1)} %get-tuple-element.27.own_ref) | copy-start | bytes 6291460
  17.8 2.9 %copy-start.5 = (s32[32,1]{0,1:T(1,128)S(1)}, s32[32,1]{0,1:T(1,128)}, u32[]{:S(2)}) copy-start(s32[32,1]{0,1:T(1,128)} %param.9) | copy-start | bytes 388
  17.9 7.4 %collective-permute-start.6 = (bf16[2,2,48,512]{3,2,1,0:T(8,128)(2,1)S(1)}, bf16[2,2,48,512]{3,2,1,0:T(8,128)(2,1)S(1)}, u32[]{:S(2)}, u32[]{:S(2)}) collective-permute-start(bf16[2,2,48,512]{3,2,1,0:T(8,128)(2,1)S(1)} %pad_maximum_fusion.7.b0), channel_id=1, source_target_pairs={{0,48},{16,32},{32,16},{48,0},{64,112},{80,96},{96,80},{112,64},{1... | collective-permute-start | bytes 589832 | tf_op jit(solution)/shard_map/ppermute | solution.py:307
  20.6 5.9 %collective-permute-start.2 = (bf16[2,2,48,512]{3,2,1,0:T(8,128)(2,1)S(1)}, bf16[2,2,48,512]{3,2,1,0:T(8,128)(2,1)S(1)}, u32[]{:S(2)}, u32[]{:S(2)}) collective-permute-start(bf16[2,2,48,512]{3,2,1,0:T(8,128)(2,1)S(1)} %pad_maximum_fusion.6.a0), channel_id=1, source_target_pairs={{0,16},{16,0},{32,48},{48,32},{64,80},{80,64},{96,112},{112,96},{1... | collective-permute-start | bytes 589832 | tf_op jit(solution)/shard_map/ppermute | solution.py:307
  25.3 13.5 %collective-permute-start.7 = (bf16[4,2,48,512]{3,2,1,0:T(8,128)(2,1)S(1)}, bf16[4,2,48,512]{3,2,1,0:T(8,128)(2,1)S(1)}, u32[]{:S(2)}, u32[]{:S(2)}) collective-permute-start(bf16[4,2,48,512]{3,2,1,0:T(8,128)(2,1)S(1)} %pad_maximum_fusion.1), channel_id=1, source_target_pairs={{0,16},{16,0},{32,48},{48,32},{64,80},{80,64},{96,112},{112,96},{1... | collective-permute-start | bytes 1179656 | tf_op jit(solution)/shard_map/ppermute | solution.py:307
  26.5 12.3 %collective-permute-start.3 = (bf16[4,2,48,512]{3,2,1,0:T(8,128)(2,1)S(1)}, bf16[4,2,48,512]{3,2,1,0:T(8,128)(2,1)S(1)}, u32[]{:S(2)}, u32[]{:S(2)}) collective-permute-start(bf16[4,2,48,512]{3,2,1,0:T(8,128)(2,1)S(1)} %pad_maximum_fusion), channel_id=1, source_target_pairs={{0,48},{16,32},{32,16},{48,0},{64,112},{80,96},{96,80},{112,64},{1... | collective-permute-start | bytes 1179656 | tf_op jit(solution)/shard_map/ppermute | solution.py:307
  36.1 1.3 copy-start.2
  37.5 1.3 copy-start.4
  46.2 20.2 %collective-permute-start.10 = (bf16[2,2,2,128,384]{4,3,1,2,0:T(8,128)(2,1)S(1)}, bf16[2,2,2,128,384]{4,3,1,2,0:T(8,128)(2,1)S(1)}, u32[]{:S(2)}, u32[]{:S(2)}) collective-permute-start(bf16[2,2,2,128,384]{4,3,1,2,0:T(8,128)(2,1)S(1)} %copy.25), channel_id=1, source_target_pairs={{0,12},{1,13},{2,14},{3,15},{4,8},{5,9},{6,10},{7,11},{8,4},{9,5},... | collective-permute-start | bytes 2359304 | tf_op jit(solution)/shard_map/ppermute | solution.py:307
  50.2 17.3 %collective-permute-start.8 = (bf16[2,2,2,128,384]{4,3,1,2,0:T(8,128)(2,1)S(1)}, bf16[2,2,2,128,384]{4,3,1,2,0:T(8,128)(2,1)S(1)}, u32[]{:S(2)}, u32[]{:S(2)}) collective-permute-start(bf16[2,2,2,128,384]{4,3,1,2,0:T(8,128)(2,1)S(1)} %copy.22), channel_id=1, source_target_pairs={{0,4},{1,5},{2,6},{3,7},{4,0},{5,1},{6,2},{7,3},{8,12},{9,13},{10,... | collective-permute-start | bytes 2359304 | tf_op jit(solution)/shard_map/ppermute | solution.py:307
  50.3 6.1 %collective-permute-start.15 = (bf16[2,2,48,512]{3,2,1,0:T(8,128)(2,1)S(1)}, bf16[2,2,48,512]{3,2,1,0:T(8,128)(2,1)S(1)}, u32[]{:S(2)}, u32[]{:S(2)}) collective-permute-start(bf16[2,2,48,512]{3,2,1,0:T(8,128)(2,1)S(1)} %pad_maximum_fusion.9.b0), channel_id=1, source_target_pairs={{0,48},{16,32},{32,16},{48,0},{64,112},{80,96},{96,80},{112,64},{1... | collective-permute-start | bytes 589832 | tf_op jit(solution)/shard_map/ppermute | solution.py:307
  51.5 5.0 %collective-permute-start.13 = (bf16[2,2,48,512]{3,2,1,0:T(8,128)(2,1)S(1)}, bf16[2,2,48,512]{3,2,1,0:T(8,128)(2,1)S(1)}, u32[]{:S(2)}, u32[]{:S(2)}) collective-permute-start(bf16[2,2,48,512]{3,2,1,0:T(8,128)(2,1)S(1)} %pad_maximum_fusion.8.a0), channel_id=1, source_target_pairs={{0,16},{16,0},{32,48},{48,32},{64,80},{80,64},{96,112},{112,96},{1... | collective-permute-start | bytes 589832 | tf_op jit(solution)/shard_map/ppermute | solution.py:307
  56.4 13.8 %collective-permute-start.16 = (bf16[4,2,48,512]{3,2,1,0:T(8,128)(2,1)S(1)}, bf16[4,2,48,512]{3,2,1,0:T(8,128)(2,1)S(1)}, u32[]{:S(2)}, u32[]{:S(2)}) collective-permute-start(bf16[4,2,48,512]{3,2,1,0:T(8,128)(2,1)S(1)} %pad_maximum_fusion.4), channel_id=1, source_target_pairs={{0,16},{16,0},{32,48},{48,32},{64,80},{80,64},{96,112},{112,96},{1... | collective-permute-start | bytes 1179656 | tf_op jit(solution)/shard_map/ppermute | solution.py:307
  56.6 13.7 %collective-permute-start.14 = (bf16[4,2,48,512]{3,2,1,0:T(8,128)(2,1)S(1)}, bf16[4,2,48,512]{3,2,1,0:T(8,128)(2,1)S(1)}, u32[]{:S(2)}, u32[]{:S(2)}) collective-permute-start(bf16[4,2,48,512]{3,2,1,0:T(8,128)(2,1)S(1)} %pad_maximum_fusion.3), channel_id=1, source_target_pairs={{0,48},{16,32},{32,16},{48,0},{64,112},{80,96},{96,80},{112,64},{1... | collective-permute-start | bytes 1179656 | tf_op jit(solution)/shard_map/ppermute | solution.py:307
  66.5 12.8 %collective-permute-start.11 = (bf16[2,2,128,384]{3,2,0,1:T(8,128)(2,1)S(1)}, bf16[2,2,128,384]{3,2,0,1:T(8,128)(2,1)S(1)}, u32[]{:S(2)}, u32[]{:S(2)}) collective-permute-start(bf16[2,2,128,384]{3,2,0,1:T(8,128)(2,1)S(1)} %fusion.1), channel_id=1, source_target_pairs={{0,4},{1,5},{2,6},{3,7},{4,0},{5,1},{6,2},{7,3},{8,12},{9,13},{10,... | collective-permute-start | bytes 1179656 | tf_op jit(solution)/shard_map/ppermute | solution.py:307
  67.6 11.9 %collective-permute-start.9 = (bf16[2,2,128,384]{3,2,0,1:T(8,128)(2,1)S(1)}, bf16[2,2,128,384]{3,2,0,1:T(8,128)(2,1)S(1)}, u32[]{:S(2)}, u32[]{:S(2)}) collective-permute-start(bf16[2,2,128,384]{3,2,0,1:T(8,128)(2,1)S(1)} %fusion), channel_id=1, source_target_pairs={{0,12},{1,13},{2,14},{3,15},{4,8},{5,9},{6,10},{7,11},{8,4},{9,5},... | collective-permute-start | bytes 1179656 | tf_op jit(solution)/shard_map/ppermute | solution.py:307
  77.7 17.6 %collective-permute-start.19 = (bf16[2,2,2,128,384]{4,3,1,2,0:T(8,128)(2,1)S(1)}, bf16[2,2,2,128,384]{4,3,1,2,0:T(8,128)(2,1)S(1)}, u32[]{:S(2)}, u32[]{:S(2)}) collective-permute-start(bf16[2,2,2,128,384]{4,3,1,2,0:T(8,128)(2,1)S(1)} %copy.33), channel_id=1, source_target_pairs={{0,12},{1,13},{2,14},{3,15},{4,8},{5,9},{6,10},{7,11},{8,4},{9,5},... | collective-permute-start | bytes 2359304 | tf_op jit(solution)/shard_map/ppermute | solution.py:307
  79.0 16.6 %collective-permute-start.17 = (bf16[2,2,2,128,384]{4,3,1,2,0:T(8,128)(2,1)S(1)}, bf16[2,2,2,128,384]{4,3,1,2,0:T(8,128)(2,1)S(1)}, u32[]{:S(2)}, u32[]{:S(2)}) collective-permute-start(bf16[2,2,2,128,384]{4,3,1,2,0:T(8,128)(2,1)S(1)} %copy.30), channel_id=1, source_target_pairs={{0,4},{1,5},{2,6},{3,7},{4,0},{5,1},{6,2},{7,3},{8,12},{9,13},{10,... | collective-permute-start | bytes 2359304 | tf_op jit(solution)/shard_map/ppermute | solution.py:307
  79.7 25.9 %collective-permute-start.12 = (bf16[2,2,128,384]{3,2,1,0:T(8,128)(2,1)S(1)}, bf16[2,2,128,384]{3,2,1,0:T(8,128)(2,1)S(1)}, u32[]{:S(2)}, u32[]{:S(2)}) collective-permute-start(bf16[2,2,128,384]{3,2,1,0:T(8,128)(2,1)S(1)} %pad_maximum_fusion.2), channel_id=1, source_target_pairs={{0,2},{1,3},{2,0},{3,1},{4,6},{5,7},{6,4},{7,5},{8,10},{9,11},{10,... | collective-permute-start | bytes 1179656 | tf_op jit(solution)/shard_map/ppermute | solution.py:307
  95.5 8.3 %collective-permute-start.20 = (bf16[2,2,128,384]{3,2,0,1:T(8,128)(2,1)S(1)}, bf16[2,2,128,384]{3,2,0,1:T(8,128)(2,1)S(1)}, u32[]{:S(2)}, u32[]{:S(2)}) collective-permute-start(bf16[2,2,128,384]{3,2,0,1:T(8,128)(2,1)S(1)} %fusion.3), channel_id=1, source_target_pairs={{0,4},{1,5},{2,6},{3,7},{4,0},{5,1},{6,2},{7,3},{8,12},{9,13},{10,... | collective-permute-start | bytes 1179656 | tf_op jit(solution)/shard_map/ppermute | solution.py:307
  95.7 8.2 %collective-permute-start.18 = (bf16[2,2,128,384]{3,2,0,1:T(8,128)(2,1)S(1)}, bf16[2,2,128,384]{3,2,0,1:T(8,128)(2,1)S(1)}, u32[]{:S(2)}, u32[]{:S(2)}) collective-permute-start(bf16[2,2,128,384]{3,2,0,1:T(8,128)(2,1)S(1)} %fusion.2), channel_id=1, source_target_pairs={{0,12},{1,13},{2,14},{3,15},{4,8},{5,9},{6,10},{7,11},{8,4},{9,5},... | collective-permute-start | bytes 1179656 | tf_op jit(solution)/shard_map/ppermute | solution.py:307
  104.2 6.7 %collective-permute-start.21 = (bf16[2,2,128,384]{3,2,1,0:T(8,128)(2,1)S(1)}, bf16[2,2,128,384]{3,2,1,0:T(8,128)(2,1)S(1)}, u32[]{:S(2)}, u32[]{:S(2)}) collective-permute-start(bf16[2,2,128,384]{3,2,1,0:T(8,128)(2,1)S(1)} %pad_maximum_fusion.5), channel_id=1, source_target_pairs={{0,2},{1,3},{2,0},{3,1},{4,6},{5,7},{6,4},{7,5},{8,10},{9,11},{10,... | collective-permute-start | bytes 1179656 | tf_op jit(solution)/shard_map/ppermute | solution.py:307
  113.2 32.9 %all-to-all-start = ((bf16[16,4,2,16,384]{4,3,2,1,0:T(8,128)(2,1)}), bf16[16,4,2,16,384]{4,3,2,1,0:T(8,128)(2,1)S(1)}, u32[]{:S(2)}, u32[]{:S(2)}) async-start(bf16[16,4,2,16,384]{4,3,2,1,0:T(8,128)(2,1)} %bitcast.29), calls=%async_computation | async-start | bytes 3145728 | tf_op jit(solution)/shard_map/all_to_all | solution.py:401

commit v3 on v2

--- a/solution.py
+++ b/solution.py
@@ -355,7 +355,7 @@
     b_last = swap(b_pass, "space", Z1)
     a_sum = a_keep[0].astype(F32) + a_in[0].astype(F32) + a_last.astype(F32)
     b_sum = b_keep[0].astype(F32) + b_in[0].astype(F32) + b_last.astype(F32)
-    return a_sum, b_sum, (a_in, b_in)
+    return a_sum, b_sum, (b_in, b_in)
 
 
 def on_device(resident, source, insertion, owners, diag_time, diag_mom):

time: 152 us -> 151 us (level)
  no operation moved by 1% of the time
where the time goes in v3:
time: 151 us; the launch traced here: 150 us
  waiting for transfers between devices  66.2 us (44%)
  Pallas kernels  39.2 us (26%)
  starting transfers between devices  35.5 us (24%)
  local copies, waits for them, and re-layouts  6.48 us (4%)
  other arithmetic  2.56 us (2%)
    ppermute x21, waiting for transfers between devices, swap(): return lax.ppermute(x, axis, [(i, i ^ bits) for i in range(n)])  44.9 us
    all_to_all x1, waiting for transfers between devices, on_device(): received = lax.all_to_all(outgoing, 'space', 0, 0, tiled=True)  21.3 us
    ppermute x21, starting transfers between devices, swap(): return lax.ppermute(x, axis, [(i, i ^ bits) for i in range(n)])  20.7 us
    pallas_call x2, Pallas kernels, resident_slices(): pl.pallas_call(functools.partial(resident_kernel, chunks), out_shape=[jax...  16 us
    pallas_call x2, Pallas kernels, partial_field(): pl.pallas_call(field_kernel, out_shape=(out,) * 4, grid_spec=pltpu.Prefet...  14.7 us
    all_to_all x1, starting transfers between devices, on_device(): received = lax.all_to_all(outgoing, 'space', 0, 0, tiled=True)  11.4 us
    pallas_call x1, Pallas kernels, contract(): pl.pallas_call(insertion_kernel, out_shape=jax.ShapeDtypeStruct((cap, par...  5.34 us
    unnamed x12, local copies, waits for them, and re-layouts  5.08 us
  transfers between devices with their start and end apart: 23, of which 9 were waited for; matrix products, arithmetic and copies ran while one was open for 3% of the time, Pallas kernels for 16%

profile of v3, /device:TPU:1, one launch (start us, length us, event | category | flops | bytes accessed | tf_op | source)
XLA Modules:
  0.0 150.4 jit_solution(1406241211175614634)
XLA Ops:
  0.0 1.4 collective-permute-start
  3.0 1.1 copy-done
  5.1 3.4 %collective-permute-start.5 = (bf16[4,48,512]{2,1,0:T(8,128)(2,1)S(1)}, bf16[4,48,512]{2,1,0:T(8,128)(2,1)S(1)}, u32[]{:S(2)}, u32[]{:S(2)}) collective-permute-start(bf16[4,48,512]{2,1,0:T(8,128)(2,1)S(1)} %get-tuple-element.22), channel_id=1, source_target_pairs={{0,65},{1,64},{2,67},{3,66},{4,69},{5,68},{6,71},{7,70},{8,73},{9,... | collective-permute-start | bytes 589832 | tf_op jit(solution)/shard_map/ppermute | solution.py:314
  8.5 8.0 %resident_slices.2 = (bf16[2,8,8,16,512]{4,3,2,1,0:T(8,128)(2,1)S(1)}, bf16[2,8,8,16,512]{4,3,2,1,0:T(8,128)(2,1)S(1)}) custom-call(s32[8]{0:T(128)S(1)} %concatenate.19.meta.after_ref.after_a.after_b, bf16[2,1024,8,256]{3,2,1,0:T(8,128)(2,1)} %res_ref.1, bf16[4,48,512]{2,1,0:T(8,128)(2,1)S(1)} %get-tuple-element.19.after_ref), custom_call_target="tpu_custom_call" | custom-call | flops 30000001024 | bytes 13000000 | tf_op jit(solution)/shard_map/resident_slices/pallas_call | solution.py:104
  16.5 1.3 copy-done.3
  17.9 2.6 %collective-permute-start.6 = (bf16[2,2,48,512]{3,2,1,0:T(8,128)(2,1)S(1)}, bf16[2,2,48,512]{3,2,1,0:T(8,128)(2,1)S(1)}, u32[]{:S(2)}, u32[]{:S(2)}) collective-permute-start(bf16[2,2,48,512]{3,2,1,0:T(8,128)(2,1)S(1)} %pad_maximum_fusion.7.b0), channel_id=1, source_target_pairs={{0,48},{16,32},{32,16},{48,0},{64,112},{80,96},{96,80},{112,64},{1... | collective-permute-start | bytes 589832 | tf_op jit(solution)/shard_map/ppermute | solution.py:307
  20.8 4.4 %collective-permute-done.6.b1 = bf16[2,2,48,512]{3,2,1,0:T(8,128)(2,1)S(1)} collective-permute-done((bf16[2,2,48,512]{3,2,1,0:T(8,128)(2,1)S(1)}, bf16[2,2,48,512]{3,2,1,0:T(8,128)(2,1)S(1)}, u32[]{:S(2)}, u32[]{:S(2)}) %collective-permute-start.6) | collective-permute-done | bytes 196640 | tf_op jit(solution)/shard_map/ppermute | solution.py:307
  25.5 1.0 collective-permute-done.2.a1
  26.5 1.6 %collective-permute-start.3 = (bf16[4,2,48,512]{3,2,1,0:T(8,128)(2,1)S(1)}, bf16[4,2,48,512]{3,2,1,0:T(8,128)(2,1)S(1)}, u32[]{:S(2)}, u32[]{:S(2)}) collective-permute-start(bf16[4,2,48,512]{3,2,1,0:T(8,128)(2,1)S(1)} %pad_maximum_fusion), channel_id=1, source_target_pairs={{0,48},{16,32},{32,16},{48,0},{64,112},{80,96},{96,80},{112,64},{1... | collective-permute-start | bytes 1179656 | tf_op jit(solution)/shard_map/ppermute | solution.py:307
  28.1 8.0 %resident_slices.3 = (bf16[2,8,8,16,512]{4,3,2,1,0:T(8,128)(2,1)S(1)}, bf16[2,8,8,16,512]{4,3,2,1,0:T(8,128)(2,1)S(1)}) custom-call(s32[8]{0:T(128)S(1)} %concatenate.19.meta.after_ref.after_a.after_b, bf16[2,1024,8,256]{3,2,1,0:T(8,128)(2,1)} %collective-permute-done.res_ref, bf16[4,48,512]{2,1,0:T(8,128)(2,1)S(1)} %get-tuple-element.19.after_ref), custom_call_target="tpu_custom_call" | custom-call | flops 30000001024 | bytes 13000000 | tf_op jit(solution)/shard_map/resident_slices/pallas_call | solution.py:104
  36.1 1.3 copy-done.2
  37.5 1.3 copy-done.4
  38.8 7.4 %field.2 = (bf16[2,2,2,128,384]{4,3,2,1,0:T(8,128)(2,1)S(1)}, bf16[2,2,2,128,384]{4,3,2,1,0:T(8,128)(2,1)S(1)}, bf16[2,2,2,128,384]{4,3,2,1,0:T(8,128)(2,1)S(1)}, bf16[2,2,2,128,384]{4,3,2,1,0:T(8,128)(2,1)S(1)}) custom-call(s32[8]{0:T(128)S(1)} %concatenate.19.meta.after_ref.after_a.after_b, bf16[2,8,8,16,512]{4,3,2,1,0:T(8,128)(2,1)} %copy-done.3, ...), custom_call_target="tpu_custom_call" | custom-call | flops 3221225472 | bytes 10000000 | tf_op jit(solution)/shard_map/field/pallas_call | solution.py:188
  46.2 3.8 %collective-permute-start.10 = (bf16[2,2,2,128,384]{4,3,1,2,0:T(8,128)(2,1)S(1)}, bf16[2,2,2,128,384]{4,3,1,2,0:T(8,128)(2,1)S(1)}, u32[]{:S(2)}, u32[]{:S(2)}) collective-permute-start(bf16[2,2,2,128,384]{4,3,1,2,0:T(8,128)(2,1)S(1)} %copy.25), channel_id=1, source_target_pairs={{0,12},{1,13},{2,14},{3,15},{4,8},{5,9},{6,10},{7,11},{8,4},{9,5},... | collective-permute-start | bytes 2359304 | tf_op jit(solution)/shard_map/ppermute | solution.py:307
  50.3 1.2 collective-permute-start.15
  51.7 4.7 %collective-permute-done.15.b1 = bf16[2,2,48,512]{3,2,1,0:T(8,128)(2,1)S(1)} collective-permute-done((bf16[2,2,48,512]{3,2,1,0:T(8,128)(2,1)S(1)}, bf16[2,2,48,512]{3,2,1,0:T(8,128)(2,1)S(1)}, u32[]{:S(2)}, u32[]{:S(2)}) %collective-permute-start.15) | collective-permute-done | bytes 196640 | tf_op jit(solution)/shard_map/ppermute | solution.py:307
  56.6 1.5 collective-permute-start.14
  58.1 8.4 %collective-permute-done.10 = bf16[2,2,2,128,384]{4,3,1,2,0:T(8,128)(2,1)S(1)} collective-permute-done((bf16[2,2,2,128,384]{4,3,1,2,0:T(8,128)(2,1)S(1)}, bf16[2,2,2,128,384]{4,3,1,2,0:T(8,128)(2,1)S(1)}, u32[]{:S(2)}, u32[]{:S(2)}) %collective-permute-start.10) | collective-permute-done | bytes 786464 | tf_op jit(solution)/shard_map/ppermute | solution.py:307
  66.6 0.9 collective-permute-done.8
  67.6 1.6 %collective-permute-start.9 = (bf16[2,2,128,384]{3,2,0,1:T(8,128)(2,1)S(1)}, bf16[2,2,128,384]{3,2,0,1:T(8,128)(2,1)S(1)}, u32[]{:S(2)}, u32[]{:S(2)}) collective-permute-start(bf16[2,2,128,384]{3,2,0,1:T(8,128)(2,1)S(1)} %fusion), channel_id=1, source_target_pairs={{0,12},{1,13},{2,14},{3,15},{4,8},{5,9},{6,10},{7,11},{8,4},{9,5},... | collective-permute-start | bytes 1179656 | tf_op jit(solution)/shard_map/ppermute | solution.py:307
  69.3 7.4 %field.3 = (bf16[2,2,2,128,384]{4,3,2,1,0:T(8,128)(2,1)S(1)}, bf16[2,2,2,128,384]{4,3,2,1,0:T(8,128)(2,1)S(1)}, bf16[2,2,2,128,384]{4,3,2,1,0:T(8,128)(2,1)S(1)}, bf16[2,2,2,128,384]{4,3,2,1,0:T(8,128)(2,1)S(1)}) custom-call(s32[8]{0:T(128)S(1)} %concatenate.19.meta.after_ref.after_a.after_b, bf16[2,8,8,16,512]{4,3,2,1,0:T(8,128)(2,1)} %copy-done.1, ...), custom_call_target="tpu_custom_call" | custom-call | flops 3221225472 | bytes 10000000 | tf_op jit(solution)/shard_map/field/pallas_call | solution.py:188
  76.8 1.2 collective-permute-start.19
  78.8 1.4 collective-permute-start.12
  80.2 14.2 %collective-permute-done.19 = bf16[2,2,2,128,384]{4,3,1,2,0:T(8,128)(2,1)S(1)} collective-permute-done((bf16[2,2,2,128,384]{4,3,1,2,0:T(8,128)(2,1)S(1)}, bf16[2,2,2,128,384]{4,3,1,2,0:T(8,128)(2,1)S(1)}, u32[]{:S(2)}, u32[]{:S(2)}) %collective-permute-start.19) | collective-permute-done | bytes 786464 | tf_op jit(solution)/shard_map/ppermute | solution.py:307
  94.8 1.8 %collective-permute-start.18 = (bf16[2,2,128,384]{3,2,0,1:T(8,128)(2,1)S(1)}, bf16[2,2,128,384]{3,2,0,1:T(8,128)(2,1)S(1)}, u32[]{:S(2)}, u32[]{:S(2)}) collective-permute-start(bf16[2,2,128,384]{3,2,0,1:T(8,128)(2,1)S(1)} %fusion.2), channel_id=1, source_target_pairs={{0,12},{1,13},{2,14},{3,15},{4,8},{5,9},{6,10},{7,11},{8,4},{9,5},... | collective-permute-start | bytes 1179656 | tf_op jit(solution)/shard_map/ppermute | solution.py:307
  96.6 6.2 %collective-permute-done.20 = bf16[2,2,128,384]{3,2,0,1:T(8,128)(2,1)S(1)} collective-permute-done((bf16[2,2,128,384]{3,2,0,1:T(8,128)(2,1)S(1)}, bf16[2,2,128,384]{3,2,0,1:T(8,128)(2,1)S(1)}, u32[]{:S(2)}, u32[]{:S(2)}) %collective-permute-start.20) | collective-permute-done | bytes 393248 | tf_op jit(solution)/shard_map/ppermute | solution.py:307
  103.2 1.4 collective-permute-start.21
  104.7 5.2 %collective-permute-done.21.refs_5_ = bf16[2,2,128,384]{3,2,1,0:T(8,128)(2,1)S(1)} collective-permute-done((bf16[2,2,128,384]{3,2,1,0:T(8,128)(2,1)S(1)}, bf16[2,2,128,384]{3,2,1,0:T(8,128)(2,1)S(1)}, u32[]{:S(2)}, u32[]{:S(2)}) %collective-permute-start.21) | collective-permute-done | bytes 393248 | tf_op jit(solution)/shard_map/ppermute | solution.py:307
  109.9 2.3 %pack.1 = bf16[64,2,16,384]{3,2,1,0:T(8,128)(2,1)} custom-call(s32[64]{0:T(128)S(1)} %select_reduce_fusion.slot_ref, f32[2,128,384]{2,1,0:T(8,128)S(1)} %slice_bitcast_fusion.3.refs_0_, f32[2,128,384]{2,1,0:T(8,128)S(1)} %slice_bitcast_fusion.2.refs_1_, bf16[2,2,128,384]{3,2,1,0:T(8,128)(2,1)S(1)} %collective-permute-done.12.refs_2_, ...), custom_call_target="tpu_custom_call" | custom-call | flops 1000000 | bytes 4000000 | tf_op jit(solution)/shard_map/pack/pallas_call | solution.py:238
  112.2 11.4 %all-to-all-start = ((bf16[16,4,2,16,384]{4,3,2,1,0:T(8,128)(2,1)}), bf16[16,4,2,16,384]{4,3,2,1,0:T(8,128)(2,1)S(1)}, u32[]{:S(2)}, u32[]{:S(2)}) async-start(bf16[16,4,2,16,384]{4,3,2,1,0:T(8,128)(2,1)} %bitcast.29), calls=%async_computation | async-start | bytes 3145728 | tf_op jit(solution)/shard_map/all_to_all | solution.py:401
  123.8 21.3 %all-to-all-done.rows_ref = bf16[16,4,2,16,384]{4,3,2,1,0:T(8,128)(2,1)S(1)} async-done(((bf16[16,4,2,16,384]{4,3,2,1,0:T(8,128)(2,1)}), bf16[16,4,2,16,384]{4,3,2,1,0:T(8,128)(2,1)S(1)}, u32[]{:S(2)}, u32[]{:S(2)}) %all-to-all-start) | async-done | bytes 1572896 | tf_op jit(solution)/shard_map/all_to_all | solution.py:401
  145.1 5.3 %contract.1 = bf16[4,2,128,1024]{3,2,1,0:T(8,128)(2,1)} custom-call(s32[4]{0:T(128)S(1)} %and_select_fusion.1.which, s32[4]{0:T(128)S(1)} %get-tuple-element.33.filled, bf16[16,4,2,16,384]{4,3,2,1,0:T(8,128)(2,1)S(1)} %all-to-all-done.rows_ref, bf16[4,8,2,48,1024]{4,3,2,1,0:T(8,128)(2,1)} %bitcast.56), custom_call_target="tpu_custom_call" | custom-call | flops 1600000000 | bytes 10000000 | tf_op jit(solution)/shard_map/contract/pallas_call | solution.py:281
  (77 shorter events, 5.9 us)
Async XLA Ops:
  0.0 28.1 %collective-permute-start = (bf16[2,1024,8,256]{3,2,1,0:T(8,128)(2,1)}, bf16[2,1024,8,256]{3,2,1,0:T(8,128)(2,1)}, u32[]{:S(2)}, u32[]{:S(2)}) collective-permute-start(bf16[2,1024,8,256]{3,2,1,0:T(8,128)(2,1)} %res_ref.1), channel_id=1, source_target_pairs={{0,1},{1,0},{2,3},{3,2},{4,5},{5,4},{6,7},{7,6},{8,9},{9,8},{10,11... | collective-permute-start | bytes 25165832 | tf_op jit(solution)/shard_map/ppermute | solution.py:307
  3.0 1.1 copy-start
  5.0 12.8 %collective-permute-start.4 = (bf16[4,48,512]{2,1,0:T(8,128)(2,1)S(1)}, bf16[4,48,512]{2,1,0:T(8,128)(2,1)S(1)}, u32[]{:S(2)}, u32[]{:S(2)}) collective-permute-start(bf16[4,48,512]{2,1,0:T(8,128)(2,1)S(1)} %get-tuple-element.22), channel_id=1, source_target_pairs={{0,1},{1,0},{2,3},{3,2},{4,5},{5,4},{6,7},{7,6},{8,9},{9,8},{10,11... | collective-permute-start | bytes 589832 | tf_op jit(solution)/shard_map/ppermute | solution.py:307
  5.1 12.8 %collective-permute-start.5 = (bf16[4,48,512]{2,1,0:T(8,128)(2,1)S(1)}, bf16[4,48,512]{2,1,0:T(8,128)(2,1)S(1)}, u32[]{:S(2)}, u32[]{:S(2)}) collective-permute-start(bf16[4,48,512]{2,1,0:T(8,128)(2,1)S(1)} %get-tuple-element.22), channel_id=1, source_target_pairs={{0,65},{1,64},{2,67},{3,66},{4,69},{5,68},{6,71},{7,70},{8,73},{9,... | collective-permute-start | bytes 589832 | tf_op jit(solution)/shard_map/ppermute | solution.py:314
  8.5 12.1 %collective-permute-start.1 = (bf16[4,48,512]{2,1,0:T(8,128)(2,1)S(1)}, bf16[4,48,512]{2,1,0:T(8,128)(2,1)S(1)}, u32[]{:S(2)}, u32[]{:S(2)}) collective-permute-start(bf16[4,48,512]{2,1,0:T(8,128)(2,1)S(1)} %get-tuple-element.19.after_ref), channel_id=1, source_target_pairs={{0,64},{16,80},{32,96},{48,112},{64,0},{80,16},{96,32},{112,48},{1... | collective-permute-start | bytes 589832 | tf_op jit(solution)/shard_map/ppermute | solution.py:307
  16.5 1.3 copy-start.3
  17.8 8.7 %copy-start.1 = (bf16[2,8,8,16,512]{4,3,2,1,0:T(8,128)(2,1)}, bf16[2,8,8,16,512]{4,3,2,1,0:T(8,128)(2,1)S(1)}, u32[]{:S(2)}) copy-start(bf16[2,8,8,16,512]{4,3,2,1,0:T(8,128)(2,1)S(1)} %get-tuple-element.27.own_ref) | copy-start | bytes 6291460
  17.8 2.9 %copy-start.5 = (s32[32,1]{0,1:T(1,128)S(1)}, s32[32,1]{0,1:T(1,128)}, u32[]{:S(2)}) copy-start(s32[32,1]{0,1:T(1,128)} %param.9) | copy-start | bytes 388
  17.9 7.4 %collective-permute-start.6 = (bf16[2,2,48,512]{3,2,1,0:T(8,128)(2,1)S(1)}, bf16[2,2,48,512]{3,2,1,0:T(8,128)(2,1)S(1)}, u32[]{:S(2)}, u32[]{:S(2)}) collective-permute-start(bf16[2,2,48,512]{3,2,1,0:T(8,128)(2,1)S(1)} %pad_maximum_fusion.7.b0), channel_id=1, source_target_pairs={{0,48},{16,32},{32,16},{48,0},{64,112},{80,96},{96,80},{112,64},{1... | collective-permute-start | bytes 589832 | tf_op jit(solution)/shard_map/ppermute | solution.py:307
  20.6 5.9 %collective-permute-start.2 = (bf16[2,2,48,512]{3,2,1,0:T(8,128)(2,1)S(1)}, bf16[2,2,48,512]{3,2,1,0:T(8,128)(2,1)S(1)}, u32[]{:S(2)}, u32[]{:S(2)}) collective-permute-start(bf16[2,2,48,512]{3,2,1,0:T(8,128)(2,1)S(1)} %pad_maximum_fusion.6.a0), channel_id=1, source_target_pairs={{0,16},{16,0},{32,48},{48,32},{64,80},{80,64},{96,112},{112,96},{1... | collective-permute-start | bytes 589832 | tf_op jit(solution)/shard_map/ppermute | solution.py:307
  25.3 13.5 %collective-permute-start.7 = (bf16[4,2,48,512]{3,2,1,0:T(8,128)(2,1)S(1)}, bf16[4,2,48,512]{3,2,1,0:T(8,128)(2,1)S(1)}, u32[]{:S(2)}, u32[]{:S(2)}) collective-permute-start(bf16[4,2,48,512]{3,2,1,0:T(8,128)(2,1)S(1)} %pad_maximum_fusion.1), channel_id=1, source_target_pairs={{0,16},{16,0},{32,48},{48,32},{64,80},{80,64},{96,112},{112,96},{1... | collective-permute-start | bytes 1179656 | tf_op jit(solution)/shard_map/ppermute | solution.py:307
  26.5 12.3 %collective-permute-start.3 = (bf16[4,2,48,512]{3,2,1,0:T(8,128)(2,1)S(1)}, bf16[4,2,48,512]{3,2,1,0:T(8,128)(2,1)S(1)}, u32[]{:S(2)}, u32[]{:S(2)}) collective-permute-start(bf16[4,2,48,512]{3,2,1,0:T(8,128)(2,1)S(1)} %pad_maximum_fusion), channel_id=1, source_target_pairs={{0,48},{16,32},{32,16},{48,0},{64,112},{80,96},{96,80},{112,64},{1... | collective-permute-start | bytes 1179656 | tf_op jit(solution)/shard_map/ppermute | solution.py:307
  36.1 1.3 copy-start.2
  37.5 1.3 copy-start.4
  46.2 20.2 %collective-permute-start.10 = (bf16[2,2,2,128,384]{4,3,1,2,0:T(8,128)(2,1)S(1)}, bf16[2,2,2,128,384]{4,3,1,2,0:T(8,128)(2,1)S(1)}, u32[]{:S(2)}, u32[]{:S(2)}) collective-permute-start(bf16[2,2,2,128,384]{4,3,1,2,0:T(8,128)(2,1)S(1)} %copy.25), channel_id=1, source_target_pairs={{0,12},{1,13},{2,14},{3,15},{4,8},{5,9},{6,10},{7,11},{8,4},{9,5},... | collective-permute-start | bytes 2359304 | tf_op jit(solution)/shard_map/ppermute | solution.py:307
  50.2 17.3 %collective-permute-start.8 = (bf16[2,2,2,128,384]{4,3,1,2,0:T(8,128)(2,1)S(1)}, bf16[2,2,2,128,384]{4,3,1,2,0:T(8,128)(2,1)S(1)}, u32[]{:S(2)}, u32[]{:S(2)}) collective-permute-start(bf16[2,2,2,128,384]{4,3,1,2,0:T(8,128)(2,1)S(1)} %copy.22), channel_id=1, source_target_pairs={{0,4},{1,5},{2,6},{3,7},{4,0},{5,1},{6,2},{7,3},{8,12},{9,13},{10,... | collective-permute-start | bytes 2359304 | tf_op jit(solution)/shard_map/ppermute | solution.py:307
  50.3 6.1 %collective-permute-start.15 = (bf16[2,2,48,512]{3,2,1,0:T(8,128)(2,1)S(1)}, bf16[2,2,48,512]{3,2,1,0:T(8,128)(2,1)S(1)}, u32[]{:S(2)}, u32[]{:S(2)}) collective-permute-start(bf16[2,2,48,512]{3,2,1,0:T(8,128)(2,1)S(1)} %pad_maximum_fusion.9.b0), channel_id=1, source_target_pairs={{0,48},{16,32},{32,16},{48,0},{64,112},{80,96},{96,80},{112,64},{1... | collective-permute-start | bytes 589832 | tf_op jit(solution)/shard_map/ppermute | solution.py:307
  51.5 5.0 %collective-permute-start.13 = (bf16[2,2,48,512]{3,2,1,0:T(8,128)(2,1)S(1)}, bf16[2,2,48,512]{3,2,1,0:T(8,128)(2,1)S(1)}, u32[]{:S(2)}, u32[]{:S(2)}) collective-permute-start(bf16[2,2,48,512]{3,2,1,0:T(8,128)(2,1)S(1)} %pad_maximum_fusion.8.a0), channel_id=1, source_target_pairs={{0,16},{16,0},{32,48},{48,32},{64,80},{80,64},{96,112},{112,96},{1... | collective-permute-start | bytes 589832 | tf_op jit(solution)/shard_map/ppermute | solution.py:307
  56.4 12.9 %collective-permute-start.16 = (bf16[4,2,48,512]{3,2,1,0:T(8,128)(2,1)S(1)}, bf16[4,2,48,512]{3,2,1,0:T(8,128)(2,1)S(1)}, u32[]{:S(2)}, u32[]{:S(2)}) collective-permute-start(bf16[4,2,48,512]{3,2,1,0:T(8,128)(2,1)S(1)} %pad_maximum_fusion.4), channel_id=1, source_target_pairs={{0,16},{16,0},{32,48},{48,32},{64,80},{80,64},{96,112},{112,96},{1... | collective-permute-start | bytes 1179656 | tf_op jit(solution)/shard_map/ppermute | solution.py:307
  56.6 12.7 %collective-permute-start.14 = (bf16[4,2,48,512]{3,2,1,0:T(8,128)(2,1)S(1)}, bf16[4,2,48,512]{3,2,1,0:T(8,128)(2,1)S(1)}, u32[]{:S(2)}, u32[]{:S(2)}) collective-permute-start(bf16[4,2,48,512]{3,2,1,0:T(8,128)(2,1)S(1)} %pad_maximum_fusion.3), channel_id=1, source_target_pairs={{0,48},{16,32},{32,16},{48,0},{64,112},{80,96},{96,80},{112,64},{1... | collective-permute-start | bytes 1179656 | tf_op jit(solution)/shard_map/ppermute | solution.py:307
  66.6 11.8 %collective-permute-start.11 = (bf16[2,2,128,384]{3,2,0,1:T(8,128)(2,1)S(1)}, bf16[2,2,128,384]{3,2,0,1:T(8,128)(2,1)S(1)}, u32[]{:S(2)}, u32[]{:S(2)}) collective-permute-start(bf16[2,2,128,384]{3,2,0,1:T(8,128)(2,1)S(1)} %fusion.1), channel_id=1, source_target_pairs={{0,4},{1,5},{2,6},{3,7},{4,0},{5,1},{6,2},{7,3},{8,12},{9,13},{10,... | collective-permute-start | bytes 1179656 | tf_op jit(solution)/shard_map/ppermute | solution.py:307
  67.6 10.9 %collective-permute-start.9 = (bf16[2,2,128,384]{3,2,0,1:T(8,128)(2,1)S(1)}, bf16[2,2,128,384]{3,2,0,1:T(8,128)(2,1)S(1)}, u32[]{:S(2)}, u32[]{:S(2)}) collective-permute-start(bf16[2,2,128,384]{3,2,0,1:T(8,128)(2,1)S(1)} %fusion), channel_id=1, source_target_pairs={{0,12},{1,13},{2,14},{3,15},{4,8},{5,9},{6,10},{7,11},{8,4},{9,5},... | collective-permute-start | bytes 1179656 | tf_op jit(solution)/shard_map/ppermute | solution.py:307
  76.8 17.6 %collective-permute-start.19 = (bf16[2,2,2,128,384]{4,3,1,2,0:T(8,128)(2,1)S(1)}, bf16[2,2,2,128,384]{4,3,1,2,0:T(8,128)(2,1)S(1)}, u32[]{:S(2)}, u32[]{:S(2)}) collective-permute-start(bf16[2,2,2,128,384]{4,3,1,2,0:T(8,128)(2,1)S(1)} %copy.33), channel_id=1, source_target_pairs={{0,12},{1,13},{2,14},{3,15},{4,8},{5,9},{6,10},{7,11},{8,4},{9,5},... | collective-permute-start | bytes 2359304 | tf_op jit(solution)/shard_map/ppermute | solution.py:307
  78.1 16.6 %collective-permute-start.17 = (bf16[2,2,2,128,384]{4,3,1,2,0:T(8,128)(2,1)S(1)}, bf16[2,2,2,128,384]{4,3,1,2,0:T(8,128)(2,1)S(1)}, u32[]{:S(2)}, u32[]{:S(2)}) collective-permute-start(bf16[2,2,2,128,384]{4,3,1,2,0:T(8,128)(2,1)S(1)} %copy.30), channel_id=1, source_target_pairs={{0,4},{1,5},{2,6},{3,7},{4,0},{5,1},{6,2},{7,3},{8,12},{9,13},{10,... | collective-permute-start | bytes 2359304 | tf_op jit(solution)/shard_map/ppermute | solution.py:307
  78.8 25.9 %collective-permute-start.12 = (bf16[2,2,128,384]{3,2,1,0:T(8,128)(2,1)S(1)}, bf16[2,2,128,384]{3,2,1,0:T(8,128)(2,1)S(1)}, u32[]{:S(2)}, u32[]{:S(2)}) collective-permute-start(bf16[2,2,128,384]{3,2,1,0:T(8,128)(2,1)S(1)} %pad_maximum_fusion.2), channel_id=1, source_target_pairs={{0,2},{1,3},{2,0},{3,1},{4,6},{5,7},{6,4},{7,5},{8,10},{9,11},{10,... | collective-permute-start | bytes 1179656 | tf_op jit(solution)/shard_map/ppermute | solution.py:307
  94.5 8.3 %collective-permute-start.20 = (bf16[2,2,128,384]{3,2,0,1:T(8,128)(2,1)S(1)}, bf16[2,2,128,384]{3,2,0,1:T(8,128)(2,1)S(1)}, u32[]{:S(2)}, u32[]{:S(2)}) collective-permute-start(bf16[2,2,128,384]{3,2,0,1:T(8,128)(2,1)S(1)} %fusion.3), channel_id=1, source_target_pairs={{0,4},{1,5},{2,6},{3,7},{4,0},{5,1},{6,2},{7,3},{8,12},{9,13},{10,... | collective-permute-start | bytes 1179656 | tf_op jit(solution)/shard_map/ppermute | solution.py:307
  94.8 8.2 %collective-permute-start.18 = (bf16[2,2,128,384]{3,2,0,1:T(8,128)(2,1)S(1)}, bf16[2,2,128,384]{3,2,0,1:T(8,128)(2,1)S(1)}, u32[]{:S(2)}, u32[]{:S(2)}) collective-permute-start(bf16[2,2,128,384]{3,2,0,1:T(8,128)(2,1)S(1)} %fusion.2), channel_id=1, source_target_pairs={{0,12},{1,13},{2,14},{3,15},{4,8},{5,9},{6,10},{7,11},{8,4},{9,5},... | collective-permute-start | bytes 1179656 | tf_op jit(solution)/shard_map/ppermute | solution.py:307
  103.2 6.7 %collective-permute-start.21 = (bf16[2,2,128,384]{3,2,1,0:T(8,128)(2,1)S(1)}, bf16[2,2,128,384]{3,2,1,0:T(8,128)(2,1)S(1)}, u32[]{:S(2)}, u32[]{:S(2)}) collective-permute-start(bf16[2,2,128,384]{3,2,1,0:T(8,128)(2,1)S(1)} %pad_maximum_fusion.5), channel_id=1, source_target_pairs={{0,2},{1,3},{2,0},{3,1},{4,6},{5,7},{6,4},{7,5},{8,10},{9,11},{10,... | collective-permute-start | bytes 1179656 | tf_op jit(solution)/shard_map/ppermute | solution.py:307
  112.2 32.9 %all-to-all-start = ((bf16[16,4,2,16,384]{4,3,2,1,0:T(8,128)(2,1)}), bf16[16,4,2,16,384]{4,3,2,1,0:T(8,128)(2,1)S(1)}, u32[]{:S(2)}, u32[]{:S(2)}) async-start(bf16[16,4,2,16,384]{4,3,2,1,0:T(8,128)(2,1)} %bitcast.29), calls=%async_computation | async-start | bytes 3145728 | tf_op jit(solution)/shard_map/all_to_all | solution.py:401

commit v4 on v3

--- a/solution.py
+++ b/solution.py
@@ -135,42 +135,43 @@
     _, groups, blocks, rows, width = own_ref.shape
     sites = width // 2
     columns = real_rhs.shape[1] * real_rhs.shape[2]
-    for side, arrays in enumerate(((a0, a1, a2), (b0, b1, b2))):
-        for ref, places in zip(arrays, PLACES[side]):
-            for n, place in enumerate(places):
-                at = me ^ place
-                v = ref[n, 0]
-                real_rhs[side, at] = v
-                imag_rhs[side, at, :, 0:sites] = v[:, sites:]
-                imag_rhs[side, at, :, sites:] = -v[:, 0:sites]
-
-    zs = groups // 2
+    @pl.when(pl.program_id(1) == 0)
+    def _():
+        for side, arrays in enumerate(((a0, a1, a2), (b0, b1, b2))):
+            for ref, places in zip(arrays, PLACES[side]):
+                for n, place in enumerate(places):
+                    at = me ^ place
+                    v = ref[n, 0]
+                    real_rhs[side, at] = v
+                    imag_rhs[side, at, :, 0:sites] = v[:, sites:]
+                    imag_rhs[side, at, :, sites:] = -v[:, 0:sites]
+
+    zs = groups
     tall = blocks * rows
-    for k in range(2):
-        left = [x[0, k * zs : (k + 1) * zs].reshape(zs * tall, width) for x in (own_ref, par_ref)]
-
-        def product(rhs, left=left):
-            total = None
-            for n, x in enumerate(left):
-                term = lax.dot_general(
-                    x,
-                    rhs[n].reshape(columns, width),
-                    (((1,), (1,)), ((), ())),
-                    preferred_element_type=F32,
-                )
-                total = term if total is None else total + term
-            return total.astype(BF).reshape(zs, tall, columns)
-
-        real = product(real_rhs)
-        imag = product(imag_rhs)
-        a_keep[0, 0, k] = real[0]
-        a_send[0, 0, k] = real[1]
-        a_send[1, 0, k] = real[2]
-        a_keep[1, 0, k] = real[3]
-        b_keep[0, 0, k] = imag[0]
-        b_keep[1, 0, k] = imag[1]
-        b_send[1, 0, k] = imag[2]
-        b_send[0, 0, k] = imag[3]
+    left = [x[0].reshape(zs * tall, width) for x in (own_ref, par_ref)]
+
+    def product(rhs, left=left):
+        total = None
+        for n, x in enumerate(left):
+            term = lax.dot_general(
+                x,
+                rhs[n].reshape(columns, width),
+                (((1,), (1,)), ((), ())),
+                preferred_element_type=F32,
+            )
+            total = term if total is None else total + term
+        return total.astype(BF).reshape(zs, tall, columns)
+
+    real = product(real_rhs)
+    imag = product(imag_rhs)
+    a_keep[0, 0, 0] = real[0]
+    a_send[0, 0, 0] = real[1]
+    a_send[1, 0, 0] = real[2]
+    a_keep[1, 0, 0] = real[3]
+    b_keep[0, 0, 0] = imag[0]
+    b_keep[1, 0, 0] = imag[1]
+    b_send[1, 0, 0] = imag[2]
+    b_send[0, 0, 0] = imag[3]
 
 
 def partial_field(n, at, meta, own, par, side_a, side_b, after_a, after_b):
@@ -179,23 +180,23 @@
     columns = 8 * modes
     out = jax.ShapeDtypeStruct((2, n, 2, blocks * rows, columns), BF)
     left = pl.BlockSpec(
-        (1, groups, blocks, rows, width), lambda i, meta: (at + i, 0, 0, 0, 0)
+        (1, groups // 2, blocks, rows, width), lambda i, k, meta: (at + i, k, 0, 0, 0)
     )
 
     def piece(x):
-        return pl.BlockSpec((x.shape[0], 1, modes, width), lambda i, meta: (0, i, 0, 0))
+        return pl.BlockSpec((x.shape[0], 1, modes, width), lambda i, k, meta: (0, i, 0, 0))
 
     return pl.pallas_call(
         field_kernel,
         out_shape=(out,) * 4,
         grid_spec=pltpu.PrefetchScalarGridSpec(
             num_scalar_prefetch=1,
-            grid=(n,),
+            grid=(n, 2),
             in_specs=[left, left]
             + [piece(x) for x in (*side_a, *side_b)]
             + [pl.BlockSpec(memory_space=pl.ANY)] * 2,
             out_specs=[
-                pl.BlockSpec((2, 1, *out.shape[2:]), lambda i, meta: (0, i, 0, 0, 0))
+                pl.BlockSpec((2, 1, 1, *out.shape[3:]), lambda i, k, meta: (0, i, k, 0, 0))
             ]
             * 4,
             scratch_shapes=[pltpu.VMEM((2, 8, modes, width), BF)] * 2,

time: 151 us -> 151 us (level)
  transfers between devices with their start and end apart: 23 -> 23, of which waited for: 9 -> 10; matrix products, arithmetic and copies ran while one was open for 3% -> 3% of each run, Pallas kernels for 16% -> 16%
where the time goes in v4:
time: 151 us; the launch traced here: 150 us
  waiting for transfers between devices  66.5 us (44%)
  Pallas kernels  39.6 us (26%)
  starting transfers between devices  34.8 us (23%)
  local copies, waits for them, and re-layouts  6.48 us (4%)
  other arithmetic  2.55 us (2%)
    ppermute x21, waiting for transfers between devices, swap(): return lax.ppermute(x, axis, [(i, i ^ bits) for i in range(n)])  45.2 us
    all_to_all x1, waiting for transfers between devices, on_device(): received = lax.all_to_all(outgoing, 'space', 0, 0, tiled=True)  21.3 us
    ppermute x21, starting transfers between devices, swap(): return lax.ppermute(x, axis, [(i, i ^ bits) for i in range(n)])  20.1 us
    pallas_call x2, Pallas kernels, resident_slices(): pl.pallas_call(functools.partial(resident_kernel, chunks), out_shape=[jax...  16 us
    pallas_call x2, Pallas kernels, partial_field(): pl.pallas_call(field_kernel, out_shape=(out,) * 4, grid_spec=pltpu.Prefet...  15.1 us
    all_to_all x1, starting transfers between devices, on_device(): received = lax.all_to_all(outgoing, 'space', 0, 0, tiled=True)  11.3 us
    pallas_call x1, Pallas kernels, contract(): pl.pallas_call(insertion_kernel, out_shape=jax.ShapeDtypeStruct((cap, par...  5.33 us
    unnamed x12, local copies, waits for them, and re-layouts  5.08 us
  transfers between devices with their start and end apart: 23, of which 10 were waited for; matrix products, arithmetic and copies ran while one was open for 3% of the time, Pallas kernels for 16%

profile of v4, /device:TPU:1, one launch (start us, length us, event | category | flops | bytes accessed | tf_op | source)
XLA Modules:
  0.0 150.4 jit_solution(164416789393016452)
XLA Ops:
  0.0 1.4 collective-permute-start
  3.0 1.1 copy-done
  5.1 3.4 %collective-permute-start.5 = (bf16[4,48,512]{2,1,0:T(8,128)(2,1)S(1)}, bf16[4,48,512]{2,1,0:T(8,128)(2,1)S(1)}, u32[]{:S(2)}, u32[]{:S(2)}) collective-permute-start(bf16[4,48,512]{2,1,0:T(8,128)(2,1)S(1)} %get-tuple-element.22), channel_id=1, source_target_pairs={{0,65},{1,64},{2,67},{3,66},{4,69},{5,68},{6,71},{7,70},{8,73},{9,... | collective-permute-start | bytes 589832 | tf_op jit(solution)/shard_map/ppermute | solution.py:315
  8.5 8.0 %resident_slices.2 = (bf16[2,8,8,16,512]{4,3,2,1,0:T(8,128)(2,1)S(1)}, bf16[2,8,8,16,512]{4,3,2,1,0:T(8,128)(2,1)S(1)}) custom-call(s32[8]{0:T(128)S(1)} %concatenate.19.meta.after_ref.after_a.after_b, bf16[2,1024,8,256]{3,2,1,0:T(8,128)(2,1)} %res_ref.1, bf16[4,48,512]{2,1,0:T(8,128)(2,1)S(1)} %get-tuple-element.19.after_ref), custom_call_target="tpu_custom_call" | custom-call | flops 30000001024 | bytes 13000000 | tf_op jit(solution)/shard_map/resident_slices/pallas_call | solution.py:104
  16.5 1.3 copy-done.3
  17.9 2.6 %collective-permute-start.6 = (bf16[2,2,48,512]{3,2,1,0:T(8,128)(2,1)S(1)}, bf16[2,2,48,512]{3,2,1,0:T(8,128)(2,1)S(1)}, u32[]{:S(2)}, u32[]{:S(2)}) collective-permute-start(bf16[2,2,48,512]{3,2,1,0:T(8,128)(2,1)S(1)} %pad_maximum_fusion.7.b0), channel_id=1, source_target_pairs={{0,48},{16,32},{32,16},{48,0},{64,112},{80,96},{96,80},{112,64},{1... | collective-permute-start | bytes 589832 | tf_op jit(solution)/shard_map/ppermute | solution.py:308
  20.8 4.4 %collective-permute-done.6.b1 = bf16[2,2,48,512]{3,2,1,0:T(8,128)(2,1)S(1)} collective-permute-done((bf16[2,2,48,512]{3,2,1,0:T(8,128)(2,1)S(1)}, bf16[2,2,48,512]{3,2,1,0:T(8,128)(2,1)S(1)}, u32[]{:S(2)}, u32[]{:S(2)}) %collective-permute-start.6) | collective-permute-done | bytes 196640 | tf_op jit(solution)/shard_map/ppermute | solution.py:308
  25.5 0.9 collective-permute-done.2.a1
  26.5 1.6 %collective-permute-start.3 = (bf16[4,2,48,512]{3,2,1,0:T(8,128)(2,1)S(1)}, bf16[4,2,48,512]{3,2,1,0:T(8,128)(2,1)S(1)}, u32[]{:S(2)}, u32[]{:S(2)}) collective-permute-start(bf16[4,2,48,512]{3,2,1,0:T(8,128)(2,1)S(1)} %pad_maximum_fusion), channel_id=1, source_target_pairs={{0,48},{16,32},{32,16},{48,0},{64,112},{80,96},{96,80},{112,64},{1... | collective-permute-start | bytes 1179656 | tf_op jit(solution)/shard_map/ppermute | solution.py:308
  28.1 8.0 %resident_slices.3 = (bf16[2,8,8,16,512]{4,3,2,1,0:T(8,128)(2,1)S(1)}, bf16[2,8,8,16,512]{4,3,2,1,0:T(8,128)(2,1)S(1)}) custom-call(s32[8]{0:T(128)S(1)} %concatenate.19.meta.after_ref.after_a.after_b, bf16[2,1024,8,256]{3,2,1,0:T(8,128)(2,1)} %collective-permute-done.res_ref, bf16[4,48,512]{2,1,0:T(8,128)(2,1)S(1)} %get-tuple-element.19.after_ref), custom_call_target="tpu_custom_call" | custom-call | flops 30000001024 | bytes 13000000 | tf_op jit(solution)/shard_map/resident_slices/pallas_call | solution.py:104
  36.1 1.3 copy-done.2
  37.5 1.3 copy-done.4
  38.8 7.6 %field.2 = (bf16[2,2,2,128,384]{4,3,2,1,0:T(8,128)(2,1)S(1)}, bf16[2,2,2,128,384]{4,3,2,1,0:T(8,128)(2,1)S(1)}, bf16[2,2,2,128,384]{4,3,2,1,0:T(8,128)(2,1)S(1)}, bf16[2,2,2,128,384]{4,3,2,1,0:T(8,128)(2,1)S(1)}) custom-call(s32[8]{0:T(128)S(1)} %concatenate.19.meta.after_ref.after_a.after_b, bf16[2,8,8,16,512]{4,3,2,1,0:T(8,128)(2,1)} %copy-done.3, ...), custom_call_target="tpu_custom_call" | custom-call | flops 3221225472 | bytes 10000000 | tf_op jit(solution)/shard_map/field/pallas_call | solution.py:189
  46.4 3.8 %collective-permute-start.10 = (bf16[2,2,2,128,384]{4,3,1,2,0:T(8,128)(2,1)S(1)}, bf16[2,2,2,128,384]{4,3,1,2,0:T(8,128)(2,1)S(1)}, u32[]{:S(2)}, u32[]{:S(2)}) collective-permute-start(bf16[2,2,2,128,384]{4,3,1,2,0:T(8,128)(2,1)S(1)} %copy.25), channel_id=1, source_target_pairs={{0,12},{1,13},{2,14},{3,15},{4,8},{5,9},{6,10},{7,11},{8,4},{9,5},... | collective-permute-start | bytes 2359304 | tf_op jit(solution)/shard_map/ppermute | solution.py:308
  50.5 1.2 collective-permute-start.15
  51.9 4.7 %collective-permute-done.15.b1 = bf16[2,2,48,512]{3,2,1,0:T(8,128)(2,1)S(1)} collective-permute-done((bf16[2,2,48,512]{3,2,1,0:T(8,128)(2,1)S(1)}, bf16[2,2,48,512]{3,2,1,0:T(8,128)(2,1)S(1)}, u32[]{:S(2)}, u32[]{:S(2)}) %collective-permute-start.15) | collective-permute-done | bytes 196640 | tf_op jit(solution)/shard_map/ppermute | solution.py:308
  56.8 1.5 collective-permute-start.14
  58.3 8.4 %collective-permute-done.10 = bf16[2,2,2,128,384]{4,3,1,2,0:T(8,128)(2,1)S(1)} collective-permute-done((bf16[2,2,2,128,384]{4,3,1,2,0:T(8,128)(2,1)S(1)}, bf16[2,2,2,128,384]{4,3,1,2,0:T(8,128)(2,1)S(1)}, u32[]{:S(2)}, u32[]{:S(2)}) %collective-permute-start.10) | collective-permute-done | bytes 786464 | tf_op jit(solution)/shard_map/ppermute | solution.py:308
  66.8 0.9 collective-permute-done.8
  67.8 1.6 %collective-permute-start.9 = (bf16[2,2,128,384]{3,2,0,1:T(8,128)(2,1)S(1)}, bf16[2,2,128,384]{3,2,0,1:T(8,128)(2,1)S(1)}, u32[]{:S(2)}, u32[]{:S(2)}) collective-permute-start(bf16[2,2,128,384]{3,2,0,1:T(8,128)(2,1)S(1)} %fusion), channel_id=1, source_target_pairs={{0,12},{1,13},{2,14},{3,15},{4,8},{5,9},{6,10},{7,11},{8,4},{9,5},... | collective-permute-start | bytes 1179656 | tf_op jit(solution)/shard_map/ppermute | solution.py:308
  69.5 7.6 %field.3 = (bf16[2,2,2,128,384]{4,3,2,1,0:T(8,128)(2,1)S(1)}, bf16[2,2,2,128,384]{4,3,2,1,0:T(8,128)(2,1)S(1)}, bf16[2,2,2,128,384]{4,3,2,1,0:T(8,128)(2,1)S(1)}, bf16[2,2,2,128,384]{4,3,2,1,0:T(8,128)(2,1)S(1)}) custom-call(s32[8]{0:T(128)S(1)} %concatenate.19.meta.after_ref.after_a.after_b, bf16[2,8,8,16,512]{4,3,2,1,0:T(8,128)(2,1)} %copy-done.1, ...), custom_call_target="tpu_custom_call" | custom-call | flops 3221225472 | bytes 10000000 | tf_op jit(solution)/shard_map/field/pallas_call | solution.py:189
  77.2 1.2 collective-permute-start.19
  79.0 1.4 collective-permute-start.12
  80.4 14.4 %collective-permute-done.19 = bf16[2,2,2,128,384]{4,3,1,2,0:T(8,128)(2,1)S(1)} collective-permute-done((bf16[2,2,2,128,384]{4,3,1,2,0:T(8,128)(2,1)S(1)}, bf16[2,2,2,128,384]{4,3,1,2,0:T(8,128)(2,1)S(1)}, u32[]{:S(2)}, u32[]{:S(2)}) %collective-permute-start.19) | collective-permute-done | bytes 786464 | tf_op jit(solution)/shard_map/ppermute | solution.py:308
  95.2 1.4 collective-permute-start.18
  96.6 6.2 %collective-permute-done.20 = bf16[2,2,128,384]{3,2,0,1:T(8,128)(2,1)S(1)} collective-permute-done((bf16[2,2,128,384]{3,2,0,1:T(8,128)(2,1)S(1)}, bf16[2,2,128,384]{3,2,0,1:T(8,128)(2,1)S(1)}, u32[]{:S(2)}, u32[]{:S(2)}) %collective-permute-start.20) | collective-permute-done | bytes 393248 | tf_op jit(solution)/shard_map/ppermute | solution.py:308
  103.3 1.4 collective-permute-start.21
  104.8 5.2 %collective-permute-done.21.refs_5_ = bf16[2,2,128,384]{3,2,1,0:T(8,128)(2,1)S(1)} collective-permute-done((bf16[2,2,128,384]{3,2,1,0:T(8,128)(2,1)S(1)}, bf16[2,2,128,384]{3,2,1,0:T(8,128)(2,1)S(1)}, u32[]{:S(2)}, u32[]{:S(2)}) %collective-permute-start.21) | collective-permute-done | bytes 393248 | tf_op jit(solution)/shard_map/ppermute | solution.py:308
  110.0 2.3 %pack.1 = bf16[64,2,16,384]{3,2,1,0:T(8,128)(2,1)} custom-call(s32[64]{0:T(128)S(1)} %select_reduce_fusion.slot_ref, f32[2,128,384]{2,1,0:T(8,128)S(1)} %slice_bitcast_fusion.3.refs_0_, f32[2,128,384]{2,1,0:T(8,128)S(1)} %slice_bitcast_fusion.2.refs_1_, bf16[2,2,128,384]{3,2,1,0:T(8,128)(2,1)S(1)} %collective-permute-done.12.refs_2_, ...), custom_call_target="tpu_custom_call" | custom-call | flops 1000000 | bytes 4000000 | tf_op jit(solution)/shard_map/pack/pallas_call | solution.py:239
  112.3 11.3 %all-to-all-start = ((bf16[16,4,2,16,384]{4,3,2,1,0:T(8,128)(2,1)}), bf16[16,4,2,16,384]{4,3,2,1,0:T(8,128)(2,1)S(1)}, u32[]{:S(2)}, u32[]{:S(2)}) async-start(bf16[16,4,2,16,384]{4,3,2,1,0:T(8,128)(2,1)} %bitcast.29), calls=%async_computation | async-start | bytes 3145728 | tf_op jit(solution)/shard_map/all_to_all | solution.py:402
  123.8 21.3 %all-to-all-done.rows_ref = bf16[16,4,2,16,384]{4,3,2,1,0:T(8,128)(2,1)S(1)} async-done(((bf16[16,4,2,16,384]{4,3,2,1,0:T(8,128)(2,1)}), bf16[16,4,2,16,384]{4,3,2,1,0:T(8,128)(2,1)S(1)}, u32[]{:S(2)}, u32[]{:S(2)}) %all-to-all-start) | async-done | bytes 1572896 | tf_op jit(solution)/shard_map/all_to_all | solution.py:402
  145.1 5.3 %contract.1 = bf16[4,2,128,1024]{3,2,1,0:T(8,128)(2,1)} custom-call(s32[4]{0:T(128)S(1)} %and_select_fusion.1.which, s32[4]{0:T(128)S(1)} %get-tuple-element.33.filled, bf16[16,4,2,16,384]{4,3,2,1,0:T(8,128)(2,1)S(1)} %all-to-all-done.rows_ref, bf16[4,8,2,48,1024]{4,3,2,1,0:T(8,128)(2,1)} %bitcast.56), custom_call_target="tpu_custom_call" | custom-call | flops 1600000000 | bytes 10000000 | tf_op jit(solution)/shard_map/contract/pallas_call | solution.py:282
  (77 shorter events, 5.8 us)
Async XLA Ops:
  0.0 28.1 %collective-permute-start = (bf16[2,1024,8,256]{3,2,1,0:T(8,128)(2,1)}, bf16[2,1024,8,256]{3,2,1,0:T(8,128)(2,1)}, u32[]{:S(2)}, u32[]{:S(2)}) collective-permute-start(bf16[2,1024,8,256]{3,2,1,0:T(8,128)(2,1)} %res_ref.1), channel_id=1, source_target_pairs={{0,1},{1,0},{2,3},{3,2},{4,5},{5,4},{6,7},{7,6},{8,9},{9,8},{10,11... | collective-permute-start | bytes 25165832 | tf_op jit(solution)/shard_map/ppermute | solution.py:308
  3.0 1.1 copy-start
  5.0 12.8 %collective-permute-start.4 = (bf16[4,48,512]{2,1,0:T(8,128)(2,1)S(1)}, bf16[4,48,512]{2,1,0:T(8,128)(2,1)S(1)}, u32[]{:S(2)}, u32[]{:S(2)}) collective-permute-start(bf16[4,48,512]{2,1,0:T(8,128)(2,1)S(1)} %get-tuple-element.22), channel_id=1, source_target_pairs={{0,1},{1,0},{2,3},{3,2},{4,5},{5,4},{6,7},{7,6},{8,9},{9,8},{10,11... | collective-permute-start | bytes 589832 | tf_op jit(solution)/shard_map/ppermute | solution.py:308
  5.1 12.8 %collective-permute-start.5 = (bf16[4,48,512]{2,1,0:T(8,128)(2,1)S(1)}, bf16[4,48,512]{2,1,0:T(8,128)(2,1)S(1)}, u32[]{:S(2)}, u32[]{:S(2)}) collective-permute-start(bf16[4,48,512]{2,1,0:T(8,128)(2,1)S(1)} %get-tuple-element.22), channel_id=1, source_target_pairs={{0,65},{1,64},{2,67},{3,66},{4,69},{5,68},{6,71},{7,70},{8,73},{9,... | collective-permute-start | bytes 589832 | tf_op jit(solution)/shard_map/ppermute | solution.py:315
  8.5 12.1 %collective-permute-start.1 = (bf16[4,48,512]{2,1,0:T(8,128)(2,1)S(1)}, bf16[4,48,512]{2,1,0:T(8,128)(2,1)S(1)}, u32[]{:S(2)}, u32[]{:S(2)}) collective-permute-start(bf16[4,48,512]{2,1,0:T(8,128)(2,1)S(1)} %get-tuple-element.19.after_ref), channel_id=1, source_target_pairs={{0,64},{16,80},{32,96},{48,112},{64,0},{80,16},{96,32},{112,48},{1... | collective-permute-start | bytes 589832 | tf_op jit(solution)/shard_map/ppermute | solution.py:308
  16.5 1.3 copy-start.3
  17.8 8.6 %copy-start.1 = (bf16[2,8,8,16,512]{4,3,2,1,0:T(8,128)(2,1)}, bf16[2,8,8,16,512]{4,3,2,1,0:T(8,128)(2,1)S(1)}, u32[]{:S(2)}) copy-start(bf16[2,8,8,16,512]{4,3,2,1,0:T(8,128)(2,1)S(1)} %get-tuple-element.27.own_ref) | copy-start | bytes 6291460
  17.8 2.9 %copy-start.5 = (s32[32,1]{0,1:T(1,128)S(1)}, s32[32,1]{0,1:T(1,128)}, u32[]{:S(2)}) copy-start(s32[32,1]{0,1:T(1,128)} %param.9) | copy-start | bytes 388
  17.9 7.4 %collective-permute-start.6 = (bf16[2,2,48,512]{3,2,1,0:T(8,128)(2,1)S(1)}, bf16[2,2,48,512]{3,2,1,0:T(8,128)(2,1)S(1)}, u32[]{:S(2)}, u32[]{:S(2)}) collective-permute-start(bf16[2,2,48,512]{3,2,1,0:T(8,128)(2,1)S(1)} %pad_maximum_fusion.7.b0), channel_id=1, source_target_pairs={{0,48},{16,32},{32,16},{48,0},{64,112},{80,96},{96,80},{112,64},{1... | collective-permute-start | bytes 589832 | tf_op jit(solution)/shard_map/ppermute | solution.py:308
  20.6 5.9 %collective-permute-start.2 = (bf16[2,2,48,512]{3,2,1,0:T(8,128)(2,1)S(1)}, bf16[2,2,48,512]{3,2,1,0:T(8,128)(2,1)S(1)}, u32[]{:S(2)}, u32[]{:S(2)}) collective-permute-start(bf16[2,2,48,512]{3,2,1,0:T(8,128)(2,1)S(1)} %pad_maximum_fusion.6.a0), channel_id=1, source_target_pairs={{0,16},{16,0},{32,48},{48,32},{64,80},{80,64},{96,112},{112,96},{1... | collective-permute-start | bytes 589832 | tf_op jit(solution)/shard_map/ppermute | solution.py:308
  25.3 13.5 %collective-permute-start.7 = (bf16[4,2,48,512]{3,2,1,0:T(8,128)(2,1)S(1)}, bf16[4,2,48,512]{3,2,1,0:T(8,128)(2,1)S(1)}, u32[]{:S(2)}, u32[]{:S(2)}) collective-permute-start(bf16[4,2,48,512]{3,2,1,0:T(8,128)(2,1)S(1)} %pad_maximum_fusion.1), channel_id=1, source_target_pairs={{0,16},{16,0},{32,48},{48,32},{64,80},{80,64},{96,112},{112,96},{1... | collective-permute-start | bytes 1179656 | tf_op jit(solution)/shard_map/ppermute | solution.py:308
  26.5 12.3 %collective-permute-start.3 = (bf16[4,2,48,512]{3,2,1,0:T(8,128)(2,1)S(1)}, bf16[4,2,48,512]{3,2,1,0:T(8,128)(2,1)S(1)}, u32[]{:S(2)}, u32[]{:S(2)}) collective-permute-start(bf16[4,2,48,512]{3,2,1,0:T(8,128)(2,1)S(1)} %pad_maximum_fusion), channel_id=1, source_target_pairs={{0,48},{16,32},{32,16},{48,0},{64,112},{80,96},{96,80},{112,64},{1... | collective-permute-start | bytes 1179656 | tf_op jit(solution)/shard_map/ppermute | solution.py:308
  36.1 1.3 copy-start.2
  37.5 1.3 copy-start.4
  46.4 20.2 %collective-permute-start.10 = (bf16[2,2,2,128,384]{4,3,1,2,0:T(8,128)(2,1)S(1)}, bf16[2,2,2,128,384]{4,3,1,2,0:T(8,128)(2,1)S(1)}, u32[]{:S(2)}, u32[]{:S(2)}) collective-permute-start(bf16[2,2,2,128,384]{4,3,1,2,0:T(8,128)(2,1)S(1)} %copy.25), channel_id=1, source_target_pairs={{0,12},{1,13},{2,14},{3,15},{4,8},{5,9},{6,10},{7,11},{8,4},{9,5},... | collective-permute-start | bytes 2359304 | tf_op jit(solution)/shard_map/ppermute | solution.py:308
  50.3 17.3 %collective-permute-start.8 = (bf16[2,2,2,128,384]{4,3,1,2,0:T(8,128)(2,1)S(1)}, bf16[2,2,2,128,384]{4,3,1,2,0:T(8,128)(2,1)S(1)}, u32[]{:S(2)}, u32[]{:S(2)}) collective-permute-start(bf16[2,2,2,128,384]{4,3,1,2,0:T(8,128)(2,1)S(1)} %copy.22), channel_id=1, source_target_pairs={{0,4},{1,5},{2,6},{3,7},{4,0},{5,1},{6,2},{7,3},{8,12},{9,13},{10,... | collective-permute-start | bytes 2359304 | tf_op jit(solution)/shard_map/ppermute | solution.py:308
  50.5 6.1 %collective-permute-start.15 = (bf16[2,2,48,512]{3,2,1,0:T(8,128)(2,1)S(1)}, bf16[2,2,48,512]{3,2,1,0:T(8,128)(2,1)S(1)}, u32[]{:S(2)}, u32[]{:S(2)}) collective-permute-start(bf16[2,2,48,512]{3,2,1,0:T(8,128)(2,1)S(1)} %pad_maximum_fusion.9.b0), channel_id=1, source_target_pairs={{0,48},{16,32},{32,16},{48,0},{64,112},{80,96},{96,80},{112,64},{1... | collective-permute-start | bytes 589832 | tf_op jit(solution)/shard_map/ppermute | solution.py:308
  51.7 5.0 %collective-permute-start.13 = (bf16[2,2,48,512]{3,2,1,0:T(8,128)(2,1)S(1)}, bf16[2,2,48,512]{3,2,1,0:T(8,128)(2,1)S(1)}, u32[]{:S(2)}, u32[]{:S(2)}) collective-permute-start(bf16[2,2,48,512]{3,2,1,0:T(8,128)(2,1)S(1)} %pad_maximum_fusion.8.a0), channel_id=1, source_target_pairs={{0,16},{16,0},{32,48},{48,32},{64,80},{80,64},{96,112},{112,96},{1... | collective-permute-start | bytes 589832 | tf_op jit(solution)/shard_map/ppermute | solution.py:308
  56.6 12.9 %collective-permute-start.16 = (bf16[4,2,48,512]{3,2,1,0:T(8,128)(2,1)S(1)}, bf16[4,2,48,512]{3,2,1,0:T(8,128)(2,1)S(1)}, u32[]{:S(2)}, u32[]{:S(2)}) collective-permute-start(bf16[4,2,48,512]{3,2,1,0:T(8,128)(2,1)S(1)} %pad_maximum_fusion.4), channel_id=1, source_target_pairs={{0,16},{16,0},{32,48},{48,32},{64,80},{80,64},{96,112},{112,96},{1... | collective-permute-start | bytes 1179656 | tf_op jit(solution)/shard_map/ppermute | solution.py:308
  56.8 12.7 %collective-permute-start.14 = (bf16[4,2,48,512]{3,2,1,0:T(8,128)(2,1)S(1)}, bf16[4,2,48,512]{3,2,1,0:T(8,128)(2,1)S(1)}, u32[]{:S(2)}, u32[]{:S(2)}) collective-permute-start(bf16[4,2,48,512]{3,2,1,0:T(8,128)(2,1)S(1)} %pad_maximum_fusion.3), channel_id=1, source_target_pairs={{0,48},{16,32},{32,16},{48,0},{64,112},{80,96},{96,80},{112,64},{1... | collective-permute-start | bytes 1179656 | tf_op jit(solution)/shard_map/ppermute | solution.py:308
  66.7 11.8 %collective-permute-start.11 = (bf16[2,2,128,384]{3,2,0,1:T(8,128)(2,1)S(1)}, bf16[2,2,128,384]{3,2,0,1:T(8,128)(2,1)S(1)}, u32[]{:S(2)}, u32[]{:S(2)}) collective-permute-start(bf16[2,2,128,384]{3,2,0,1:T(8,128)(2,1)S(1)} %fusion.1), channel_id=1, source_target_pairs={{0,4},{1,5},{2,6},{3,7},{4,0},{5,1},{6,2},{7,3},{8,12},{9,13},{10,... | collective-permute-start | bytes 1179656 | tf_op jit(solution)/shard_map/ppermute | solution.py:308
  67.8 10.9 %collective-permute-start.9 = (bf16[2,2,128,384]{3,2,0,1:T(8,128)(2,1)S(1)}, bf16[2,2,128,384]{3,2,0,1:T(8,128)(2,1)S(1)}, u32[]{:S(2)}, u32[]{:S(2)}) collective-permute-start(bf16[2,2,128,384]{3,2,0,1:T(8,128)(2,1)S(1)} %fusion), channel_id=1, source_target_pairs={{0,12},{1,13},{2,14},{3,15},{4,8},{5,9},{6,10},{7,11},{8,4},{9,5},... | collective-permute-start | bytes 1179656 | tf_op jit(solution)/shard_map/ppermute | solution.py:308
  77.2 17.6 %collective-permute-start.19 = (bf16[2,2,2,128,384]{4,3,1,2,0:T(8,128)(2,1)S(1)}, bf16[2,2,2,128,384]{4,3,1,2,0:T(8,128)(2,1)S(1)}, u32[]{:S(2)}, u32[]{:S(2)}) collective-permute-start(bf16[2,2,2,128,384]{4,3,1,2,0:T(8,128)(2,1)S(1)} %copy.33), channel_id=1, source_target_pairs={{0,12},{1,13},{2,14},{3,15},{4,8},{5,9},{6,10},{7,11},{8,4},{9,5},... | collective-permute-start | bytes 2359304 | tf_op jit(solution)/shard_map/ppermute | solution.py:308
  78.5 16.6 %collective-permute-start.17 = (bf16[2,2,2,128,384]{4,3,1,2,0:T(8,128)(2,1)S(1)}, bf16[2,2,2,128,384]{4,3,1,2,0:T(8,128)(2,1)S(1)}, u32[]{:S(2)}, u32[]{:S(2)}) collective-permute-start(bf16[2,2,2,128,384]{4,3,1,2,0:T(8,128)(2,1)S(1)} %copy.30), channel_id=1, source_target_pairs={{0,4},{1,5},{2,6},{3,7},{4,0},{5,1},{6,2},{7,3},{8,12},{9,13},{10,... | collective-permute-start | bytes 2359304 | tf_op jit(solution)/shard_map/ppermute | solution.py:308
  79.0 25.8 %collective-permute-start.12 = (bf16[2,2,128,384]{3,2,1,0:T(8,128)(2,1)S(1)}, bf16[2,2,128,384]{3,2,1,0:T(8,128)(2,1)S(1)}, u32[]{:S(2)}, u32[]{:S(2)}) collective-permute-start(bf16[2,2,128,384]{3,2,1,0:T(8,128)(2,1)S(1)} %pad_maximum_fusion.2), channel_id=1, source_target_pairs={{0,2},{1,3},{2,0},{3,1},{4,6},{5,7},{6,4},{7,5},{8,10},{9,11},{10,... | collective-permute-start | bytes 1179656 | tf_op jit(solution)/shard_map/ppermute | solution.py:308
  94.9 7.9 %collective-permute-start.20 = (bf16[2,2,128,384]{3,2,0,1:T(8,128)(2,1)S(1)}, bf16[2,2,128,384]{3,2,0,1:T(8,128)(2,1)S(1)}, u32[]{:S(2)}, u32[]{:S(2)}) collective-permute-start(bf16[2,2,128,384]{3,2,0,1:T(8,128)(2,1)S(1)} %fusion.3), channel_id=1, source_target_pairs={{0,4},{1,5},{2,6},{3,7},{4,0},{5,1},{6,2},{7,3},{8,12},{9,13},{10,... | collective-permute-start | bytes 1179656 | tf_op jit(solution)/shard_map/ppermute | solution.py:308
  95.2 7.9 %collective-permute-start.18 = (bf16[2,2,128,384]{3,2,0,1:T(8,128)(2,1)S(1)}, bf16[2,2,128,384]{3,2,0,1:T(8,128)(2,1)S(1)}, u32[]{:S(2)}, u32[]{:S(2)}) collective-permute-start(bf16[2,2,128,384]{3,2,0,1:T(8,128)(2,1)S(1)} %fusion.2), channel_id=1, source_target_pairs={{0,12},{1,13},{2,14},{3,15},{4,8},{5,9},{6,10},{7,11},{8,4},{9,5},... | collective-permute-start | bytes 1179656 | tf_op jit(solution)/shard_map/ppermute | solution.py:308
  103.3 6.7 %collective-permute-start.21 = (bf16[2,2,128,384]{3,2,1,0:T(8,128)(2,1)S(1)}, bf16[2,2,128,384]{3,2,1,0:T(8,128)(2,1)S(1)}, u32[]{:S(2)}, u32[]{:S(2)}) collective-permute-start(bf16[2,2,128,384]{3,2,1,0:T(8,128)(2,1)S(1)} %pad_maximum_fusion.5), channel_id=1, source_target_pairs={{0,2},{1,3},{2,0},{3,1},{4,6},{5,7},{6,4},{7,5},{8,10},{9,11},{10,... | collective-permute-start | bytes 1179656 | tf_op jit(solution)/shard_map/ppermute | solution.py:308
  112.3 32.8 %all-to-all-start = ((bf16[16,4,2,16,384]{4,3,2,1,0:T(8,128)(2,1)}), bf16[16,4,2,16,384]{4,3,2,1,0:T(8,128)(2,1)S(1)}, u32[]{:S(2)}, u32[]{:S(2)}) async-start(bf16[16,4,2,16,384]{4,3,2,1,0:T(8,128)(2,1)} %bitcast.29), calls=%async_computation | async-start | bytes 3145728 | tf_op jit(solution)/shard_map/all_to_all | solution.py:402
